TPU v7x, 256 devices: a whole 4x4x8 slice. The times are simulated.
256 devices in a mesh: fsdp: 64 (over x, z, core), dp: 4 (over y).
Axes of the slice: x: 4, y: 4, z: 8, core: 2. Of those that a mesh axis runs over, the one named last changes fastest.
Arguments:
- tokens: bfloat16 [512, 7168], P(('fsdp', 'dp')), may hold values from -6 to 6
- grad_out: bfloat16 [512, 7168], P(('fsdp', 'dp')), may hold values from -1.5 to 1.5
- gate_codes: bfloat16 [7168, 16384], P('dp', 'fsdp'), may hold values from -4 to 4
- gate_scales: bfloat16 [56, 128], P('dp', 'fsdp'), may hold values from 0.003540039 to 0.03540039
- up_codes: bfloat16 [7168, 16384], P('dp', 'fsdp'), may hold values from -4 to 4
- up_scales: bfloat16 [56, 128], P('dp', 'fsdp'), may hold values from 0.003540039 to 0.03540039
- down_codes: bfloat16 [16384, 7168], P('fsdp', 'dp'), may hold values from -4 to 4
- down_scales: bfloat16 [128, 56], P('fsdp', 'dp'), may hold values from 0.0023345947 to 0.0234375
- gate_enter: bfloat16 [7168, 64], replicated, may hold values from -0.0625 to 0.0625
- gate_leave: bfloat16 [64, 16384], P(None, 'fsdp'), may hold values from -0.375 to 0.375
- up_enter: bfloat16 [7168, 64], replicated, may hold values from -0.0625 to 0.0625
- up_leave: bfloat16 [64, 16384], P(None, 'fsdp'), may hold values from -0.375 to 0.375
- down_enter: bfloat16 [16384, 64], P('fsdp'), may hold values from -0.046875 to 0.046875
- down_leave: bfloat16 [64, 7168], replicated, may hold values from -0.375 to 0.375
Outputs:
- layer_out: bfloat16 [512, 7168], P(('fsdp', 'dp'))
- grad_tokens: bfloat16 [512, 7168], P(('fsdp', 'dp'))
- d_gate_enter: float32 [7168, 64], P('fsdp')
- d_gate_leave: float32 [64, 16384], P(None, 'fsdp')
- d_up_enter: float32 [7168, 64], P('fsdp')
- d_up_leave: float32 [64, 16384], P(None, 'fsdp')
- d_down_enter: float32 [16384, 64], P('fsdp')
- d_down_leave: float32 [64, 7168], P(None, 'fsdp')
All inputs are finite; a program needn't handle non-finite values.
Results may differ from a plain program's by a relative error of at most 0.015.
Values may be sent and summed in bfloat16 or wider, within the bound.
A program may use at most 128 MiB of HBM per device.

v0:
```python
import jax
import jax.numpy as jnp
from jax import lax
from jax.sharding import PartitionSpec as P

BLOCK = 128


def dequant(codes, scales):
    rows, cols = codes.shape
    tiles = codes.reshape(rows // BLOCK, BLOCK, cols // BLOCK, BLOCK)
    tiles = tiles * scales[:, None, :, None]
    return tiles.reshape(rows, cols)


def unpack(fetched):
    return (
        dequant(fetched[0], fetched[1]),
        dequant(fetched[2], fetched[3]),
        dequant(fetched[4], fetched[5]),
    )


def mult(a, b):
    return jnp.dot(a, b, preferred_element_type=jnp.float32)


def contract_last(a, b):
    return lax.dot_general(a, b, (((1,), (1,)), ((), ())), preferred_element_type=jnp.float32)


def inner_rows(a, b):
    return lax.dot_general(a, b, (((0,), (0,)), ((), ())), preferred_element_type=jnp.float32)


def on_device(
    tokens,
    grad_out,
    gate_codes,
    gate_scales,
    up_codes,
    up_scales,
    down_codes,
    down_scales,
    gate_enter,
    gate_leave,
    up_enter,
    up_leave,
    down_enter,
    down_leave,
):
    fetched = (
        lax.all_gather(gate_codes, "dp", axis=0, tiled=True),
        lax.all_gather(gate_scales, "dp", axis=0, tiled=True),
        lax.all_gather(up_codes, "dp", axis=0, tiled=True),
        lax.all_gather(up_scales, "dp", axis=0, tiled=True),
        lax.all_gather(down_codes, "dp", axis=1, tiled=True),
        lax.all_gather(down_scales, "dp", axis=1, tiled=True),
    )
    gate_weight, up_weight, down_weight = unpack(fetched)
    own_count = tokens.shape[0]
    mine = lax.axis_index("fsdp") * own_count
    gate_own = mult(tokens, gate_enter).astype(jnp.bfloat16)
    up_own = mult(tokens, up_enter).astype(jnp.bfloat16)
    whole, gate_in, up_in = (
        lax.all_gather(tokens, "fsdp", axis=0, tiled=True),
        lax.all_gather(gate_own, "fsdp", axis=0, tiled=True),
        lax.all_gather(up_own, "fsdp", axis=0, tiled=True),
    )
    gate = mult(whole, gate_weight) + mult(gate_in, gate_leave)
    up = mult(whole, up_weight) + mult(up_in, up_leave)
    sigma = jax.nn.sigmoid(gate)
    active = gate * sigma
    hidden = (active * up).astype(jnp.bfloat16)
    down_mid = lax.psum(mult(hidden, down_enter), "fsdp").astype(jnp.bfloat16)
    out_rows = lax.psum_scatter(mult(hidden, down_weight), "fsdp", scatter_dimension=0, tiled=True)
    mid_own = lax.dynamic_slice_in_dim(down_mid, mine, own_count, 0)
    layer_out = (out_rows + mult(mid_own, down_leave)).astype(jnp.bfloat16)
    again = (
        lax.all_gather(gate_codes, "dp", axis=0, tiled=True),
        lax.all_gather(gate_scales, "dp", axis=0, tiled=True),
        lax.all_gather(up_codes, "dp", axis=0, tiled=True),
        lax.all_gather(up_scales, "dp", axis=0, tiled=True),
        lax.all_gather(down_codes, "dp", axis=1, tiled=True),
        lax.all_gather(down_scales, "dp", axis=1, tiled=True),
    )
    gate_weight, up_weight, down_weight = unpack(again)
    back_own = contract_last(grad_out, down_leave).astype(jnp.bfloat16)
    grad_whole, back_mid = (
        lax.all_gather(grad_out, "fsdp", axis=0, tiled=True),
        lax.all_gather(back_own, "fsdp", axis=0, tiled=True),
    )
    grad_hidden = contract_last(grad_whole, down_weight) + contract_last(back_mid, down_enter)
    grad_gate = (grad_hidden * up * sigma * (1.0 + gate * (1.0 - sigma))).astype(jnp.bfloat16)
    grad_up = (grad_hidden * active).astype(jnp.bfloat16)
    gate_sum, up_sum = lax.psum(
        (contract_last(grad_gate, gate_leave), contract_last(grad_up, up_leave)), "fsdp"
    )
    gate_back = gate_sum.astype(jnp.bfloat16)
    up_back = up_sum.astype(jnp.bfloat16)
    input_rows = lax.psum_scatter(
        contract_last(grad_gate, gate_weight) + contract_last(grad_up, up_weight),
        "fsdp",
        scatter_dimension=0,
        tiled=True,
    )
    gate_back_own = lax.dynamic_slice_in_dim(gate_back, mine, own_count, 0)
    up_back_own = lax.dynamic_slice_in_dim(up_back, mine, own_count, 0)
    grad_tokens = (
        input_rows + contract_last(gate_back_own, gate_enter) + contract_last(up_back_own, up_enter)
    ).astype(jnp.bfloat16)
    d_gate_leave = inner_rows(gate_in, grad_gate)
    d_up_leave = inner_rows(up_in, grad_up)
    d_down_enter = inner_rows(hidden, back_mid)
    share = gate_enter.shape[0] // lax.axis_size("fsdp")
    first = lax.axis_index("fsdp") * share
    token_cols = lax.dynamic_slice_in_dim(whole, first, share, 1)
    grad_cols = lax.dynamic_slice_in_dim(grad_whole, first, share, 1)
    totals = (
        lax.psum(inner_rows(token_cols, gate_back).astype(jnp.bfloat16), "dp").astype(jnp.float32),
        lax.psum(inner_rows(token_cols, up_back).astype(jnp.bfloat16), "dp").astype(jnp.float32),
        lax.psum(inner_rows(down_mid, grad_cols).astype(jnp.bfloat16), "dp").astype(jnp.float32),
        lax.psum(d_gate_leave.astype(jnp.bfloat16), "dp").astype(jnp.float32),
        lax.psum(d_up_leave.astype(jnp.bfloat16), "dp").astype(jnp.float32),
        lax.psum(d_down_enter.astype(jnp.bfloat16), "dp").astype(jnp.float32),
    )
    return (
        layer_out,
        grad_tokens,
        totals[0],
        totals[3],
        totals[1],
        totals[4],
        totals[5],
        totals[2],
    )


def solution(mesh):
    return jax.shard_map(
        on_device,
        mesh=mesh,
        in_specs=(
            P(("fsdp", "dp"), None),
            P(("fsdp", "dp"), None),
            P("dp", "fsdp"),
            P("dp", "fsdp"),
            P("dp", "fsdp"),
            P("dp", "fsdp"),
            P("fsdp", "dp"),
            P("fsdp", "dp"),
            P(),
            P(None, "fsdp"),
            P(),
            P(None, "fsdp"),
            P("fsdp", None),
            P(),
        ),
        out_specs=(
            P(("fsdp", "dp"), None),
            P(("fsdp", "dp"), None),
            P("fsdp", None),
            P(None, "fsdp"),
            P("fsdp", None),
            P(None, "fsdp"),
            P("fsdp", None),
            P(None, "fsdp"),
        ),
        check_vma=False,
    )
```

profile of v0, /device:TPU:7, one launch (start us, length us, event | category | flops | bytes accessed | tf_op | source)
XLA Modules:
  0.0 830.4 jit_solution(13854287210464040110)
XLA Ops:
  7.3 0.7 all-gather.20.cloned.1.call-update
  8.0 0.7 all-gather.22.cloned.1.call-update
  8.8 0.7 all-gather.16.cloned.1.call-update
  9.5 0.5 all-gather.14.cloned.1.call-update
  10.1 0.5 all-gather.18.cloned.1.call-update
  10.7 8.1 all-gather.3
  18.8 0.1 copy.34
  19.0 5.4 all-gather
  24.5 0.1 copy.31
  24.6 7.1 all-gather.5
  31.7 0.1 reshape.45
  31.8 1.6 fusion.6
  33.4 47.0 %all-gather.4 = bf16[64,2,64]{2,1,0:T(2,128)(2,1)S(1)} all-gather(bf16[1,2,64]{2,1,0:T(2,128)(2,1)S(1)} %fusion.6), channel_id=1, replica_groups=mesh['fsdp'=64,'dp'=4] {'fsdp'}, dimensions={0}, use_global_device_ids=true | all-gather | bytes 16640 | tf_op jit(solution)/shard_map/all_gather | solution.py:68
  80.4 0.3 fusion.5
  80.7 37.3 %all-gather.2 = bf16[64,2,64]{2,1,0:T(2,128)(2,1)S(1)} all-gather(bf16[1,2,64]{2,1,0:T(2,128)(2,1)S(1)} %fusion.5), channel_id=1, replica_groups=mesh['fsdp'=64,'dp'=4] {'fsdp'}, dimensions={0}, use_global_device_ids=true | all-gather | bytes 16640 | tf_op jit(solution)/shard_map/all_gather | solution.py:67
  118.0 0.3 fusion.7
  118.3 37.9 %all-gather.7 = bf16[64,2,64]{2,1,0:T(2,128)(2,1)S(1)} all-gather(bf16[1,2,64]{2,1,0:T(2,128)(2,1)S(1)} %fusion.7), channel_id=1, replica_groups=mesh['fsdp'=64,'dp'=4] {'fsdp'}, dimensions={0}, use_global_device_ids=true | all-gather | bytes 16640 | tf_op jit(solution)/shard_map/all_gather | solution.py:91
  156.2 0.2 fusion.24
  156.4 0.2 fusion.23
  156.6 0.2 fusion.25
  156.9 4.1 reshape.29
  161.0 6.8 all-gather.22.cloned.1.call-done
  167.8 4.9 reshape.47
  172.7 41.6 %all-gather.16.cloned.1.call-done = bf16[7168,256]{1,0:T(8,128)(2,1)} async-done(((bf16[1792,256]{1,0:T(8,128)(2,1)}), bf16[7168,256]{1,0:T(8,128)(2,1)}) %all-gather.16.cloned.1.call-update) | async-done | bytes 3670032 | tf_op jit(solution)/shard_map/all_gather | solution.py:55
  214.3 2.0 mul.76
  216.3 1.9 copy-done.1
  218.1 2.1 fusion.3
  220.3 42.5 %all-gather.14.cloned.1.call-done = bf16[7168,256]{1,0:T(8,128)(2,1)} async-done(((bf16[1792,256]{1,0:T(8,128)(2,1)}), bf16[7168,256]{1,0:T(8,128)(2,1)}) %all-gather.14.cloned.1.call-update) | async-done | bytes 3670032 | tf_op jit(solution)/shard_map/all_gather | solution.py:53
  262.7 2.0 mul.72
  264.7 1.8 copy-done.5
  266.6 2.1 fusion.4
  268.7 42.5 %all-gather.18.cloned.1.call-done = bf16[256,7168]{1,0:T(8,128)(2,1)} async-done(((bf16[256,1792]{1,0:T(8,128)(2,1)}), bf16[256,7168]{1,0:T(8,128)(2,1)}) %all-gather.18.cloned.1.call-update) | async-done | bytes 3670032 | tf_op jit(solution)/shard_map/all_gather | solution.py:57
  311.1 0.5 mul.80
  311.7 2.8 copy-done.8
  314.5 2.6 multiply_convert_fusion
  317.1 0.1 fusion.26
  317.3 0.8 convolution_convert_fusion
  318.1 0.1 fusion.28
  318.2 0.8 convolution_convert_fusion.1
  319.0 0.1 fusion.27
  319.2 0.8 convolution_convert_fusion.2
  320.0 215.9 %all-reduce.2 = (bf16[128,64]{0,1:T(8,128)(2,1)S(1)}, bf16[128,64]{0,1:T(8,128)(2,1)S(1)}, bf16[128,64]{0,1:T(8,128)(2,1)S(1)}) all-reduce(f32[128,64]{0,1:T(8,128)S(1)} %fusion.26, f32[128,64]{0,1:T(8,128)S(1)} %fusion.27, f32[128,64]{0,1:T(8,128)S(1)} %fusion.28), channel_id=1, replica_groups=mesh['fsdp'=64,'dp'=4] {'fsdp'}, use_global_device_ids=true, to_apply=%region_1.0 | all-reduce | flops 24576 | bytes 147456 | tf_op jit(solution)/shard_map/psum | solution.py:75
  535.9 0.8 convolution_convert_fusion.3
  536.7 0.8 convolution_convert_fusion.4
  537.5 1.7 convolution_convert_fusion.5
  539.2 0.2 all-reduce.8.cloned.1.call-start
  539.4 4.6 fusion.8
  544.1 0.6 copy-done.7
  544.7 3.3 convolution_add_fusion
  548.0 1.2 copy-done.9
  549.2 2.8 fusion.9
  552.0 0.6 copy-done.19
  552.7 0.6 dynamic-slice
  553.9 58.0 %all-reduce.10.cloned.1.call-done = (bf16[112,64]{0,1:T(8,128)(2,1)}, bf16[64,256]{1,0:T(8,128)(2,1)}, bf16[112,64]{0,1:T(8,128)(2,1)}, bf16[64,256]{1,0:T(8,128...) async-done(((bf16[112,64]{0,1:T(8,128)(2,1)}, bf16[64,256]{1,0:T(8,128)(2,1)}, bf16[112,64]{0,1:T(8,128)(2,1)}, bf16[64,256]{1,0:T(8,128)(2,1)}, ...) | async-done | bytes 141328 | tf_op jit(solution)/shard_map/psum | solution.py:120
  611.9 1.4 convert_element_type.83
  613.3 1.4 convert_element_type.87
  614.7 1.4 convert_element_type.89
  616.1 1.3 convert_element_type.81
  617.4 1.3 convert_element_type.85
  618.8 1.3 convert_element_type.91
  620.1 199.2 %all-reduce.8.cloned.1.call-done = (f32[128,7168]{1,0:T(8,128)}, f32[128,7168]{1,0:T(8,128)}) async-done(((f32[128,7168]{1,0:T(8,128)}, f32[128,7168]{1,0:T(8,128)}), (f32[128,7168]{1,0:T(8,128)}, f32[128,7168]{1,0:T(8,128)})) %all-reduce.8.cloned.1.call-update) | async-done | bytes 7340048
  819.3 1.3 convolution_add_fusion.2
  820.6 1.0 fusion.1
  821.6 1.9 fusion
  (50 shorter events, 0.5 us)
Async XLA Ops:
  7.2 73.2 %copy-start = (bf16[7168,64]{0,1:T(8,128)(2,1)S(1)}, bf16[7168,64]{0,1:T(8,128)(2,1)}, u32[]{:S(2)}) copy-start(bf16[7168,64]{0,1:T(8,128)(2,1)} %param.22) | copy-start | bytes 2752516
  7.2 73.2 %copy-start.17 = (bf16[2,7168]{1,0:T(2,128)(2,1)S(1)}, bf16[2,7168]{1,0:T(2,128)(2,1)}, u32[]{:S(2)}) copy-start(bf16[2,7168]{1,0:T(2,128)(2,1)} %param.14) | copy-start | bytes 86020
  7.2 110.8 %copy-start.18 = (bf16[2,7168]{1,0:T(2,128)(2,1)S(1)}, bf16[2,7168]{1,0:T(2,128)(2,1)}, u32[]{:S(2)}) copy-start(bf16[2,7168]{1,0:T(2,128)(2,1)} %param.15) | copy-start | bytes 86020
  7.2 110.8 %copy-start.12 = (bf16[64,7168]{1,0:T(8,128)(2,1)S(1)}, bf16[64,7168]{1,0:T(8,128)(2,1)}, u32[]{:S(2)}) copy-start(bf16[64,7168]{1,0:T(8,128)(2,1)} %param.27) | copy-start | bytes 2752516
  7.2 149.0 %copy-start.15 = (bf16[64,256]{1,0:T(8,128)(2,1)S(1)}, bf16[64,256]{1,0:T(8,128)(2,1)}, u32[]{:S(2)}) copy-start(bf16[64,256]{1,0:T(8,128)(2,1)} %param.25) | copy-start | bytes 98308
  7.2 149.2 %copy-start.16 = (bf16[64,256]{1,0:T(8,128)(2,1)S(1)}, bf16[64,256]{1,0:T(8,128)(2,1)}, u32[]{:S(2)}) copy-start(bf16[64,256]{1,0:T(8,128)(2,1)} %param.23) | copy-start | bytes 98308
  7.2 149.4 %copy-start.14 = (bf16[256,64]{0,1:T(8,128)(2,1)S(1)}, bf16[256,64]{0,1:T(8,128)(2,1)}, u32[]{:S(2)}) copy-start(bf16[256,64]{0,1:T(8,128)(2,1)} %param.26) | copy-start | bytes 98308
  7.2 149.6 %all-gather.20.cloned.1.call-start = ((), (), s32[]{:S(2)}) async-start(), calls=%async_computation.3 | async-start | bytes 1863680 | tf_op jit(solution)/shard_map/all_gather | solution.py:66
  8.0 159.8 %all-gather.22.cloned.1.call-start = ((), (), s32[]{:S(2)}) async-start(), calls=%async_computation.4 | async-start | bytes 1863680 | tf_op jit(solution)/shard_map/all_gather | solution.py:90
  8.7 205.5 %all-gather.16.cloned.1.call-start = ((), (), s32[]{:S(2)}) async-start(), calls=%async_computation.1 | async-start | bytes 4587520 | tf_op jit(solution)/shard_map/all_gather | solution.py:55
  9.5 253.3 %all-gather.14.cloned.1.call-start = ((), (), s32[]{:S(2)}) async-start(), calls=%async_computation | async-start | bytes 4587520 | tf_op jit(solution)/shard_map/all_gather | solution.py:53
  10.0 301.1 %all-gather.18.cloned.1.call-start = ((), (), s32[]{:S(2)}) async-start(), calls=%async_computation.2 | async-start | bytes 4587520 | tf_op jit(solution)/shard_map/all_gather | solution.py:57
  10.6 601.3 %all-reduce.10.cloned.1.call-start = ((), (), s32[]{:S(2)}) async-start(), calls=%async_computation.6 | async-start | bytes 294912 | tf_op jit(solution)/shard_map/psum | solution.py:120
  214.3 3.9 copy-start.6
  216.2 1.9 copy-start.1
  262.7 3.8 copy-start.10
  264.7 1.8 copy-start.5
  266.5 45.1 %copy-start.20 = (f32[128,256]{0,1:T(8,128)S(1)}, f32[128,256]{0,1:T(8,128)}, u32[]{:S(2)}) copy-start(f32[128,256]{0,1:T(8,128)} %fusion.3) | copy-start | bytes 393220
  311.1 3.4 copy-start.8
  311.7 5.5 copy-start.3
  539.2 280.1 %all-reduce.8.cloned.1.call-start = ((), (), s32[]{:S(2)}) async-start(), calls=%async_computation.5 | async-start | bytes 14680064
  539.4 4.7 copy-start.2
  539.4 5.3 copy-start.7
  544.7 3.3 copy-start.4
  544.7 4.5 copy-start.9
  552.0 0.7 copy-start.19
  552.0 268.6 %copy-start.11 = (bf16[7168,64]{0,1:T(8,128)(2,1)S(1)}, bf16[7168,64]{0,1:T(8,128)(2,1)}, u32[]{:S(2)}) copy-start(bf16[7168,64]{0,1:T(8,128)(2,1)} %param.24) | copy-start | bytes 2752516
  552.0 269.6 %copy-start.13 = (bf16[64,7168]{1,0:T(8,128)(2,1)S(1)}, bf16[64,7168]{1,0:T(8,128)(2,1)}, u32[]{:S(2)}) copy-start(bf16[64,7168]{1,0:T(8,128)(2,1)} %param.27) | copy-start | bytes 2752516
Sparse Core Ops, SparseCore 0:
  10.8 79.4 all-gather.19
  92.9 74.7 all-gather.21
  169.6 44.6 all-gather.15
  215.9 46.7 all-gather.13
  264.4 46.7 all-gather.17
  539.3 72.5 all-reduce.9
  616.1 203.1 all-reduce.7
where the time goes:
time: 833 us; the launch traced here: 830 us
  waiting for transfers between devices  394 us (47%)
  blocking collectives  359 us (43%)
  matrix products  30.7 us (4%)
  local copies, waits for them, and re-layouts  23.6 us (3%)
  between operations  15 us (2%)
    psum x1, blocking collectives, on_device(): down_mid = lax.psum(mult(hidden, down_enter), 'fsdp').astype(jnp.bfloat16)  216 us
    unnamed x8, waiting for transfers between devices  202 us
    psum x1, waiting for transfers between devices, on_device(): lax.psum(inner_rows(token_cols, gate_back).astype(jnp.bfloat16), 'dp')  58 us
    all_gather x1, blocking collectives, on_device(): lax.all_gather(up_own, 'fsdp', axis=0, tiled=True)  47 us
    all_gather x1, waiting for transfers between devices, on_device(): lax.all_gather(gate_codes, 'dp', axis=0, tiled=True)  42.5 us
    all_gather x1, waiting for transfers between devices, on_device(): lax.all_gather(down_codes, 'dp', axis=1, tiled=True)  42.5 us
    all_gather x1, waiting for transfers between devices, on_device(): lax.all_gather(up_codes, 'dp', axis=0, tiled=True)  41.6 us
    all_gather x1, blocking collectives, on_device(): lax.all_gather(back_own, 'fsdp', axis=0, tiled=True)  37.9 us
  transfers between devices with their start and end apart: 7, of which 6 were waited for; matrix products, arithmetic and copies ran while one was open for 5% of the time, Pallas kernels for 0%

commit v1 on v0

v1 whole, which is shorter than its diff:
```python
import jax
import jax.numpy as jnp
from jax import lax
from jax.experimental import pallas as pl
from jax.experimental.pallas import tpu as pltpu
from jax.sharding import PartitionSpec as P

NX, NZ, NY = 4, 8, 4
KP, KE, EX = 1792, 1920, 128
G, H, R = 16, 256, 64
NB = 384
BF, F32 = jnp.bfloat16, jnp.float32
MESH = pl.DeviceIdType.MESH
ORDER = (0, 7, 1, 6, 2, 5, 3, 4)


def mm(a, b):
    return jnp.dot(a, b, preferred_element_type=F32)


def mm_nt(a, b):
    return lax.dot_general(a, b, (((1,), (1,)), ((), ())), preferred_element_type=F32)


def mm_tn(a, b):
    return lax.dot_general(a, b, (((0,), (0,)), ((), ())), preferred_element_type=F32)


def kernel(
    send_ref, sc_ref, gc_hbm, uc_hbm, dc_hbm, gl_ref, ul_ref, de_ref, ge_hbm, ue_hbm, dl_hbm,
    rows_out, dge_out, due_out, ddl_out, dgl_out, dul_out, dde_out,
    gcv, ucv, dcv, gev, uev, dlv, ldsem,
    st1, s1s, s1r,
    wgu, wd, wss, wsr,
    aa, ags, agx, agr,
    ext, extp, exs, exr,
    part, gus, rgu, gur,
    parth, hs, rh, hr,
    hb, hbs, hall, hallr,
    gb, gbs, gall, gallr,
    po, rss, rsss, rsr, rsrs,
    xs, xss, xr, xrs,
    msg, msgs, rowsr, rowss,
    smx, sm1, sm2, t0s, t0r, t1s, t1r,
    res, mb, fd, t3s, t3r,
    dlp, dlr, dep, der, las, lar,
):
    f = lax.axis_index("fsdp")
    y = lax.axis_index("dp")
    x = lax.div(f, 16)
    z = lax.rem(lax.div(f, 2), 8)
    c = lax.rem(f, 2)
    o = 1 - c

    def fid(xx, zz, cc):
        return xx * 16 + zz * 2 + cc

    def m4(v):
        return lax.rem(v, 4)

    def m8(v):
        return lax.rem(v, 8)

    def rcopy(src, dst, ssem, rsem, ff, yy):
        return pltpu.make_async_remote_copy(
            src_ref=src, dst_ref=dst, send_sem=ssem, recv_sem=rsem,
            device_id={"fsdp": ff, "dp": yy}, device_id_type=MESH,
        )

    def wait(ref, sem):
        pltpu.make_async_copy(ref, ref, sem).wait()

    pending = []

    def send(src, dst, ssem, rsem, ff, yy, own=None):
        if own is None:
            rcopy(src, dst, ssem, rsem, ff, yy).start()
            pending.append((src, ssem, None))
            return
        away = jnp.logical_not(own)

        @pl.when(own)
        def _():
            pltpu.make_async_copy(src, dst, rsem).start()

        @pl.when(away)
        def _():
            rcopy(src, dst, ssem, rsem, ff, yy).start()

        pending.append((src, ssem, away))

    def drain():
        for src, ssem, cond in pending:
            if cond is None:
                wait(src, ssem)
            else:
                @pl.when(cond)
                def _(src=src, ssem=ssem):
                    wait(src, ssem)
        pending.clear()

    loads = [
        pltpu.make_async_copy(gc_hbm, gcv, ldsem.at[0]),
        pltpu.make_async_copy(uc_hbm, ucv, ldsem.at[1]),
        pltpu.make_async_copy(dc_hbm, dcv, ldsem.at[2]),
        pltpu.make_async_copy(ge_hbm.at[pl.ds(y * KP, KP)], gev, ldsem.at[3]),
        pltpu.make_async_copy(ue_hbm.at[pl.ds(y * KP, KP)], uev, ldsem.at[4]),
        pltpu.make_async_copy(dl_hbm.at[:, pl.ds(pl.multiple_of(y * KP, 128), KP)], dlv, ldsem.at[5]),
    ]
    for ld in loads:
        ld.start()

    barrier = pltpu.get_barrier_semaphore()
    peers = []
    for dy in range(NY):
        for dc in range(2):
            if dy or dc:
                peers.append((fid(x, z, lax.rem(c + dc, 2)), m4(y + dy)))
    for dx in range(1, NX):
        for dc in range(2):
            peers.append((fid(m4(x + dx), z, lax.rem(c + dc, 2)), y))
    for dz in range(1, NZ):
        peers.append((fid(x, m8(z + dz), c), y))
    for ff, yy in peers:
        pl.semaphore_signal(barrier, inc=1, device_id={"fsdp": ff, "dp": yy}, device_id_type=MESH)
    pl.semaphore_wait(barrier, len(peers))

    for dy in (2, 1, 3, 0):
        for kind in range(2):
            yy = m4(y + dy)
            send(
                send_ref.at[kind, yy], st1.at[y * 2 + c], s1s.at[kind * 4 + dy], s1r.at[y * 2 + c],
                fid(x, z, kind), yy, own=(c == kind) if dy == 0 else None,
            )

    def dequant_cols(codes, slot, s0):
        def body(i, carry):
            rows = pl.ds(pl.multiple_of(i * 128, 128), 128)
            wgu[slot, rows, 0:128] = (codes[rows, 0:128].astype(F32) * sc_ref[i, s0]).astype(BF)
            wgu[slot, rows, 128:256] = (codes[rows, 128:256].astype(F32) * sc_ref[i, s0 + 1]).astype(BF)
            return carry

        lax.fori_loop(0, 14, body, 0)

    sib = fid(x, z, o)
    loads[0].wait()
    dequant_cols(gcv, c, 0)
    wgu[c, KP : KP + R, :] = gl_ref[...]
    wgu[c, KP + R :, :] = jnp.zeros((R, H), BF)
    send(wgu.at[c], wgu.at[c], wss.at[0], wsr.at[0], sib, y)
    loads[1].wait()
    dequant_cols(ucv, 2 + c, 2)
    wgu[2 + c, KP : KP + R, :] = jnp.zeros((R, H), BF)
    wgu[2 + c, KP + R :, :] = ul_ref[...]
    send(wgu.at[2 + c], wgu.at[2 + c], wss.at[1], wsr.at[1], sib, y)
    loads[2].wait()

    def dequant_down(i, carry):
        cols = pl.ds(pl.multiple_of(i * 128, 128), 128)
        wd[c, 0:128, cols] = (dcv[0:128, cols].astype(F32) * sc_ref[i, 4]).astype(BF)
        wd[c, 128:256, cols] = (dcv[128:256, cols].astype(F32) * sc_ref[i, 5]).astype(BF)
        return carry

    lax.fori_loop(0, 14, dequant_down, 0)
    wd[c, :, KP:KE] = jnp.zeros((H, EX), BF)
    wd[c, :, KP : KP + R] = de_ref[...]
    send(wd.at[c], wd.at[c], wss.at[2], wsr.at[2], sib, y)

    for i in range(8):
        wait(st1.at[i], s1r.at[i])
    got = st1[...].reshape(128, H)
    row8 = lax.broadcasted_iota(jnp.int32, (G, 128), 0) * 8
    col = lax.broadcasted_iota(jnp.int32, (G, 128), 1)
    for j in range(8):
        pick = (col == row8 + j).astype(F32).astype(BF)
        v = mm(pick, got).astype(BF)
        if j < 7:
            aa[z, x, :, j * 256 : (j + 1) * 256] = v
        else:
            aa[z, x, :, KP:KE] = v[:, :EX]

    flag = jnp.where(y == 0, 1.0, 0.0).astype(F32)

    def masked(v):
        return (v.astype(F32) * flag).astype(BF)

    def have(zz, xx):
        wait(aa.at[zz, xx], agr.at[zz * 4 + xx])

    def fwd(zz, xx, tz, tx, ssem):
        send(aa.at[zz, xx], aa.at[zz, xx], ssem, agr.at[zz * 4 + xx], fid(tx, tz, c), y)

    zr, zl = m8(z + 1), m8(z + 7)
    xrt, xlt = m4(x + 1), m4(x + 3)
    xf, zf = m4(x + 2), m8(z + 4)

    def weights():
        wait(wgu.at[o], wsr.at[0])
        wait(wgu.at[2 + o], wsr.at[1])
        wait(wd.at[o], wsr.at[2])

    def front0(zs):
        def body(b, carry):
            a = jnp.concatenate([aa[zz].reshape(64, KE) for zz in zs], axis=0)
            acc = mm(a[:, :KP], wgu[b, 0:KP, :]) + mm(masked(a[:, KP:]), wgu[b, KP:KE, :])
            acc = acc.astype(BF)
            for i, zz in enumerate(zs):
                part[zz, :, b] = acc[i * 64 : (i + 1) * 64].reshape(4, G, H)
            return carry

        lax.fori_loop(0, 4, body, 0)
        for zz in zs:
            cc, q = lax.div(zz, 4), m4(zz)
            for xx in range(NX):
                yy = m4(zz + xx)
                send(
                    part.at[zz, xx], rgu.at[y, q], gus.at[zz * 4 + xx], gur.at[y * 4 + q],
                    fid(x, z, cc), yy, own=jnp.logical_and(yy == y, cc == 0),
                )

    def front1(xx):
        def body(b, carry):
            a = aa[:, xx].reshape(128, KE)
            acc = mm_nt(a[:, :KP], wd[b, :, 0:KP]) + mm_nt(masked(a[:, KP:]), wd[b, :, KP:KE])
            parth[xx, :, b] = acc.astype(BF).reshape(8, G, H)
            return carry

        lax.fori_loop(0, 2, body, 0)
        for zz in range(NZ):
            cc, q, yy = zz // 4, zz % 4, m4(xx + zz)
            send(
                parth.at[xx, zz], rh.at[y, q], hs.at[xx * 8 + zz], hr.at[y * 4 + q],
                fid(x, z, cc), yy, own=(yy == y) if cc == 1 else None,
            )

    @pl.when(c == 0)
    def _():
        keep = len(pending)
        before = pending[:]
        pending.clear()
        fwd(z, x, z, xrt, ags.at[2, z * 4 + x])
        fwd(z, x, z, xlt, ags.at[3, z * 4 + x])
        fwd(z, x, z, xf, agx)
        fwd(z, x, zr, x, ags.at[0, z * 4 + x])
        fwd(z, x, zl, x, ags.at[1, z * 4 + x])
        for xx in (xrt, xlt, xf):
            have(z, xx)
            fwd(z, xx, zr, x, ags.at[0, z * 4 + xx])
            fwd(z, xx, zl, x, ags.at[1, z * 4 + xx])
        weights()
        front0([z])
        for k in range(1, 4):
            za, zb = m8(z + 8 - k), m8(z + k)
            for i, xx in enumerate((x, xrt, xlt, xf)):
                have(za, xx)
                if k < 3 or i < 2:
                    fwd(za, xx, zr, x, ags.at[0, za * 4 + xx])
                have(zb, xx)
                if k < 3 or i >= 2:
                    fwd(zb, xx, zl, x, ags.at[1, zb * 4 + xx])
            front0([za, zb])
        for xx in range(NX):
            have(zf, xx)
        front0([zf])
        drain()
        pending.extend(before)

    @pl.when(c == 1)
    def _():
        before = pending[:]
        pending.clear()
        fwd(z, x, zr, x, ags.at[0, z * 4 + x])
        fwd(z, x, zl, x, ags.at[1, z * 4 + x])

        def spread(zz):
            fwd(zz, x, z, xrt, ags.at[2, zz * 4 + x])
            fwd(zz, x, z, xlt, ags.at[3, zz * 4 + x])

        def xstep(i):
            zz = m8(z + ORDER[i])
            have(zz, xlt)
            if i % 2 == 0:
                fwd(zz, xlt, z, xrt, ags.at[2, zz * 4 + xlt])
            have(zz, xrt)
            if i % 2 == 1:
                fwd(zz, xrt, z, xlt, ags.at[3, zz * 4 + xrt])

        spread(z)
        for k in range(1, 4):
            za, zb = m8(z + 8 - k), m8(z + k)
            have(za, x)
            fwd(za, x, zr, x, ags.at[0, za * 4 + x])
            spread(za)
            have(zb, x)
            if k < 3:
                fwd(zb, x, zl, x, ags.at[1, zb * 4 + x])
            spread(zb)
            for i in {1: (0,), 2: (1, 2), 3: (3, 4)}[k]:
                xstep(i)
        have(zf, x)
        spread(zf)
        weights()
        front1(x)
        for i in (5, 6, 7):
            xstep(i)
        front1(xlt)
        front1(xrt)
        for zz in range(NZ):
            have(zz, xf)
        front1(xf)
        drain()
        pending.extend(before)

    send(aa.at[:, :, :, pl.ds(KP, EX)], ext, exs, exr, sib, y)

    def middle(q, carry):
        for s in range(NY):
            wait(rgu.at[s, q], gur.at[s * 4 + q])
            wait(rh.at[s, q], hr.at[s * 4 + q])
        for b in range(2):
            g = rgu[0, q, b].astype(F32)
            u = rgu[0, q, 2 + b].astype(F32)
            h = rh[0, q, b].astype(F32)
            for s in range(1, NY):
                g += rgu[s, q, b].astype(F32)
                u += rgu[s, q, 2 + b].astype(F32)
                h += rh[s, q, b].astype(F32)
            sig = jax.nn.sigmoid(g)
            act = g * sig
            hb[q, b] = (act * u).astype(BF)
            gb[q, b] = (h * u * sig * (1.0 + g * (1.0 - sig))).astype(BF)
            gb[q, 2 + b] = (h * act).astype(BF)
        return carry

    lax.fori_loop(0, 4, middle, 0)
    for dy in (2, 1, 3, 0):
        yy = m4(y + dy)
        send(gb, gall.at[c * 4 + y], gbs.at[dy], gallr.at[c * 4 + y], fid(x, z, 1), yy,
             own=(c == 1) if dy == 0 else None)
        send(hb, hall.at[c * 4 + y], hbs.at[dy], hallr.at[c * 4 + y], fid(x, z, 0), yy,
             own=(c == 0) if dy == 0 else None)

    wait(ext, exr)
    for i in range(8):
        for q in range(4):
            zz = (i // 4) * 4 + q
            extp[(i * 4 + q) * G : (i * 4 + q + 1) * G, :] = ext[zz, (i % 4 + 8 - zz) % 4]

    def ring(d, slot, v, tgt):
        rss[d, slot] = v.astype(BF)
        send(rss.at[d, slot], rsr.at[d, slot], rsss.at[d, slot], rsrs.at[d, slot], tgt, y)

    def come(d, slot):
        wait(rsr.at[d, slot], rsrs.at[d, slot])
        return rsr[d, slot].astype(F32)

    def total(n):
        v = xr[0].astype(F32)
        for i in range(1, n):
            v += xr[i].astype(F32)
        return v

    def pack(fin):
        m = lax.broadcasted_iota(jnp.int32, (128, G), 0)
        r8 = lax.broadcasted_iota(jnp.int32, (128, G), 1) * 8
        acc = jnp.zeros((128, H), F32)
        for j in range(7):
            put = (m == r8 + j).astype(F32).astype(BF)
            acc += mm(put, fin[:, j * 256 : (j + 1) * 256])
        msg[...] = acc.astype(BF).reshape(8, G, H)

    @pl.when(c == 0)
    def _():
        before = pending[:]
        pending.clear()
        for i in range(8):
            wait(hall.at[i], hallr.at[i])

        def out0(ts):
            def rows(kb):
                return jnp.concatenate(
                    [hall[lax.div(t, 4) * 4 + m4(t + xx), m4(t), kb] for t in ts for xx in range(NX)], axis=0
                )

            def body(nb, carry):
                cols = pl.ds(pl.multiple_of(nb * NB, 128), NB)
                po[0 : 64 * len(ts), cols] = mm(rows(0), wd[0, :, cols]) + mm(rows(1), wd[1, :, cols])
                return carry

            lax.fori_loop(0, KE // NB, body, 0)

        right, left = fid(x, zr, 0), fid(x, zl, 0)
        out0([zf])
        for xx in range(2):
            ring(0, xx, po[xx * G : (xx + 1) * G, :], right)
            ring(1, xx + 2, po[(xx + 2) * G : (xx + 3) * G, :], left)
        for b in range(2):
            grad = mm_tn(hall[:, :, b].reshape(512, H), extp[...])
            dep[b] = grad
        send(dep.at[1], der, las.at[0], lar.at[0], sib, y)
        dde_out[...] = dep[0][:, :R]
        for s in range(1, 4):
            out0([m8(z + 4 - s), m8(z + 4 + s)])
            for xx in range(NX):
                v = po[xx * G : (xx + 1) * G, :]
                if s > 1 or xx < 2:
                    v = v + come(0, (s - 1) * 4 + xx)
                ring(0, s * 4 + xx, v, right)
                v = po[(4 + xx) * G : (5 + xx) * G, :]
                if s > 1 or xx >= 2:
                    v = v + come(1, (s - 1) * 4 + xx)
                ring(1, s * 4 + xx, v, left)
        out0([z])
        for xx in range(NX):
            v = po[xx * G : (xx + 1) * G, :] + come(0, 12 + xx) + come(1, 12 + xx)
            xs[xx] = v.astype(BF)
            send(xs.at[xx], xr.at[x], xss.at[xx], xrs.at[x], fid(xx, z, 0), y, own=(x == xx))
        loads[5].wait()
        for i in range(NX):
            wait(xr.at[i], xrs.at[i])
        fin = total(NX)
        mid = fin[:, KP:KE].astype(BF)
        smx[...] = mid
        pack((fin[:, :KP] + mm(mid[:, :R], dlv[...])).astype(BF))
        loads[3].wait()
        loads[4].wait()
        drain()
        pending.extend(before)

    @pl.when(c == 1)
    def _():
        before = pending[:]
        pending.clear()
        for i in range(8):
            wait(gall.at[i], gallr.at[i])

        def out1(t):
            def rows(b):
                return jnp.concatenate(
                    [gall[(zz // 4) * 4 + m4(t + zz), zz % 4, b] for zz in range(NZ)], axis=0
                )

            def body(nb, carry):
                cols = pl.ds(pl.multiple_of(nb * NB, 128), NB)
                acc = mm_nt(rows(0), wgu[0, cols, :])
                for b in range(1, 4):
                    acc += mm_nt(rows(b), wgu[b, cols, :])
                po[:, cols] = acc
                return carry

            lax.fori_loop(0, KE // NB, body, 0)

        right, left = fid(xrt, z, 1), fid(xlt, z, 1)
        out1(xf)
        for zz in range(4):
            ring(0, zz, po[zz * G : (zz + 1) * G, :], right)
            ring(1, zz + 4, po[(zz + 4) * G : (zz + 5) * G, :], left)
        out1(xrt)
        for zz in range(NZ):
            v = po[zz * G : (zz + 1) * G, :]
            if zz < 4:
                v = v + come(0, zz)
            ring(0, 8 + zz, v, right)
        out1(xlt)
        for zz in range(NZ):
            v = po[zz * G : (zz + 1) * G, :]
            if zz >= 4:
                v = v + come(1, zz)
            ring(1, 8 + zz, v, left)
        for b in range(4):
            grad = mm_tn(extp[...], gall[:, :, b].reshape(512, H))
            dlp[b] = grad[0:R] if b < 2 else grad[R:EX]
        send(dlp.at[0], dlr.at[0], las.at[0], lar.at[0], sib, y)
        send(dlp.at[2], dlr.at[1], las.at[1], lar.at[1], sib, y)
        dgl_out[...] = dlp[1]
        dul_out[...] = dlp[3]
        out1(x)
        for zz in range(NZ):
            v = po[zz * G : (zz + 1) * G, :] + come(0, 8 + zz) + come(1, 8 + zz)
            xs[zz] = v.astype(BF)
            send(xs.at[zz], xr.at[z], xss.at[zz], xrs.at[z], fid(x, zz, 1), y, own=(z == zz))
        loads[3].wait()
        loads[4].wait()
        for i in range(NZ):
            wait(xr.at[i], xrs.at[i])
        fin = total(NZ)
        mid = fin[:, KP:KE].astype(BF)
        smx[...] = mid
        back = mm_nt(mid[:, :R], gev[...]) + mm_nt(mid[:, R:], uev[...])
        pack((fin[:, :KP] + back).astype(BF))
        loads[5].wait()
        drain()
        pending.extend(before)

    send(smx, sm1.at[x], t0s, t0r.at[x], fid(y, z, o), y)
    for dy in (2, 1, 3, 0):
        for cc in range(2):
            yy = m4(y + dy)
            send(
                msg.at[yy * 2 + cc], rowsr.at[c, y], msgs.at[dy * 2 + cc], rowss.at[c, y],
                fid(x, z, cc), yy, own=(c == cc) if dy == 0 else None,
            )

    @pl.when(x == y)
    def _():
        before = pending[:]
        pending.clear()
        for i in range(NX):
            wait(sm1.at[i], t0r.at[i])
        for dz in (4, 3, 5, 2, 6, 1, 7):
            send(sm1, sm2.at[z], t1s.at[dz], t1r.at[z], fid(x, m8(z + dz), c), y)
        sm2[z] = sm1[...]
        for dz in range(1, NZ):
            zz = m8(z + dz)
            wait(sm2.at[zz], t1r.at[zz])
        small = sm2[...].reshape(512, EX)

        def body(nb, carry):
            cols = pl.ds(pl.multiple_of(nb * 256, 128), 256)
            res[pl.ds(pl.multiple_of(nb * 256, 128), 256), :] = mm_tn(
                aa[:, :, :, cols].reshape(512, 256), small
            )
            return carry

        lax.fori_loop(0, 7, body, 0)
        for cc in range(2):
            mb[cc] = res[pl.ds(pl.multiple_of(z * 224 + cc * 112, 8), 112), :].astype(BF)
        for dy in (2, 1, 3, 0):
            for cc in range(2):
                send(
                    mb.at[cc], fd.at[c], t3s.at[dy * 2 + cc], t3r.at[c], fid(x, z, cc), m4(y + dy),
                    own=(c == cc) if dy == 0 else None,
                )
        drain()
        pending.extend(before)

    @pl.when(c == 0)
    def _():
        wait(dlr.at[0], lar.at[0])
        wait(dlr.at[1], lar.at[1])
        dgl_out[...] = dlr[0]
        dul_out[...] = dlr[1]

    @pl.when(c == 1)
    def _():
        wait(der, lar.at[0])
        dde_out[...] = der[:, :R]

    for k in range(2):
        for s in range(NY):
            wait(rowsr.at[k, s], rowss.at[k, s])
    rows_out[...] = rowsr[...]
    wait(fd.at[0], t3r.at[0])
    wait(fd.at[1], t3r.at[1])
    v = fd[0].astype(F32)
    dge_out[...] = v[:, :R]
    due_out[...] = v[:, R:]
    ddl_out[...] = fd[1].astype(F32)
    drain()


def dma(*shape):
    return pltpu.SemaphoreType.DMA(shape)


def on_device(
    tokens, grad_out, gate_codes, gate_scales, up_codes, up_scales, down_codes, down_scales,
    gate_enter, gate_leave, up_enter, up_leave, down_enter, down_leave,
):
    gate_own = mm(tokens, gate_enter).astype(BF)
    up_own = mm(tokens, up_enter).astype(BF)
    back_own = mm_nt(grad_out, down_leave).astype(BF)
    ext = jnp.stack(
        [jnp.concatenate([gate_own, up_own], 1), jnp.concatenate([back_own, jnp.zeros_like(back_own)], 1)]
    )
    body = jnp.stack([tokens, grad_out]).reshape(2, 2, NY, KP)
    ext = jnp.broadcast_to(ext[:, :, None, :], (2, 2, NY, EX))
    pad = jnp.zeros((2, 2, NY, 2048 - KE), BF)
    sends = jnp.concatenate([body, ext, pad], axis=-1).transpose(0, 2, 1, 3).reshape(2, NY, G, H)
    scales = jnp.concatenate([gate_scales, up_scales, down_scales.T], axis=1).astype(F32)

    vm = pl.BlockSpec(memory_space=pltpu.VMEM)
    sm = pl.BlockSpec(memory_space=pltpu.SMEM)
    hb = pl.BlockSpec(memory_space=pl.ANY)
    V = pltpu.VMEM
    scratch = [
        V((KP, H), BF), V((KP, H), BF), V((H, KP), BF), V((KP, R), BF), V((KP, R), BF), V((R, KP), BF), dma(6),
        V((8, G, H), BF), dma(8), dma(8),
        V((4, KE, H), BF), V((2, H, KE), BF), dma(3), dma(3),
        V((NZ, NX, G, KE), BF), dma(4, 32), pltpu.SemaphoreType.DMA, dma(32),
        V((NZ, NX, G, EX), BF), V((512, EX), BF), pltpu.SemaphoreType.DMA, pltpu.SemaphoreType.DMA,
        V((NZ, NX, 4, G, H), BF), dma(32), V((NY, 4, 4, G, H), BF), dma(16),
        V((NX, NZ, 2, G, H), BF), dma(32), V((NY, 4, 2, G, H), BF), dma(16),
        V((4, 2, G, H), BF), dma(4), V((8, 4, 2, G, H), BF), dma(8),
        V((4, 4, G, H), BF), dma(4), V((8, 4, 4, G, H), BF), dma(8),
        V((128, KE), F32), V((2, 16, G, KE), BF), dma(2, 16), V((2, 16, G, KE), BF), dma(2, 16),
        V((8, G, KE), BF), dma(8), V((8, G, KE), BF), dma(8),
        V((8, G, H), BF), dma(8), V((2, NY, G, H), BF), dma(2, NY),
        V((G, EX), BF), V((NX, G, EX), BF), V((NZ, NX, G, EX), BF),
        pltpu.SemaphoreType.DMA, dma(NX), dma(NZ), dma(NZ),
        V((KP, EX), F32), V((2, 112, EX), BF), V((2, 112, EX), BF), dma(8), dma(2),
        V((4, R, H), F32), V((2, R, H), F32), V((2, H, EX), F32), V((H, EX), F32), dma(2), dma(2),
    ]
    S = jax.ShapeDtypeStruct
    rows, dge, due, ddl, dgl, dul, dde = pl.pallas_call(
        kernel,
        out_shape=[
            S((2, NY, G, H), BF), S((112, R), F32), S((112, R), F32), S((112, EX), F32),
            S((R, H), F32), S((R, H), F32), S((H, R), F32),
        ],
        in_specs=[vm, sm, hb, hb, hb, vm, vm, vm, hb, hb, hb],
        out_specs=[vm] * 7,
        scratch_shapes=scratch,
        compiler_params=pltpu.CompilerParams(
            collective_id=0, has_side_effects=True, vmem_limit_bytes=48 * 1024 * 1024
        ),
        name="lora_ffn_step",
    )(
        sends, scales, gate_codes, up_codes, down_codes, gate_leave, up_leave, down_enter,
        gate_enter, up_enter, down_leave,
    )
    rows = rows.reshape(2, NY, 2, 2048)[..., :KP].transpose(0, 2, 1, 3).reshape(2, 2, NY * KP)
    return rows[0], rows[1], dge, dgl, due, dul, dde, ddl[:, :R].T


def solution(mesh):
    return jax.shard_map(
        on_device,
        mesh=mesh,
        in_specs=(
            P(("fsdp", "dp"), None),
            P(("fsdp", "dp"), None),
            P("dp", "fsdp"),
            P("dp", "fsdp"),
            P("dp", "fsdp"),
            P("dp", "fsdp"),
            P("fsdp", "dp"),
            P("fsdp", "dp"),
            P(),
            P(None, "fsdp"),
            P(),
            P(None, "fsdp"),
            P("fsdp", None),
            P(),
        ),
        out_specs=(
            P(("fsdp", "dp"), None),
            P(("fsdp", "dp"), None),
            P("fsdp", None),
            P(None, "fsdp"),
            P("fsdp", None),
            P(None, "fsdp"),
            P("fsdp", None),
            P(None, "fsdp"),
        ),
        check_vma=False,
    )
```

time: 833 us -> 110 us (0.13)
  waiting for transfers between devices: 394 us -> 0 us
  blocking collectives: 359 us -> 0 us
  Pallas kernels: 0 us -> 91.3 us
  matrix products: 30.7 us -> 3.56 us
  between operations: 15 us -> 0.84 us
  local copies, waits for them, and re-layouts: 23.6 us -> 12.6 us
    psum x1 -> x0, blocking collectives: 216 us -> none  [on_device(): down_mid = lax.psum(mult(hidden, down_enter), 'fsdp').astype(jnp.bfloat16)]
    unnamed x8 -> x0, waiting for transfers between devices: 202 us -> none
    all_gather x6 -> x0, blocking collectives: 143 us -> none  [the longest x1 47 us: on_device(): lax.all_gather(up_own, 'fsdp', axis=0, tiled=True)]
    all_gather x5 -> x0, waiting for transfers between devices: 133 us -> none  [the longest x1 42.5 us: on_device(): lax.all_gather(gate_codes, 'dp', axis=0, tiled=True)]
    pallas_call x0 -> x1, Pallas kernels: none -> 91.3 us  [on_device(): pl.pallas_call(kernel, out_shape=[S((2, NY, G, H), BF), S((112, R), F32),...]
    psum x1 -> x0, waiting for transfers between devices: 58 us -> none  [on_device(): lax.psum(inner_rows(token_cols, gate_back).astype(jnp.bfloat16), 'dp')]
    dot_general x24 -> x3, matrix products: 30.7 us -> 3.56 us  [the longest x2 1.91 us: mm(): return jnp.dot(a, b, preferred_element_type=F32)]
    unnamed x50 -> x40, local copies, waits for them, and re-layouts: 19.1 us -> 11.7 us
  transfers between devices with their start and end apart: 7 -> 0, of which waited for: 6 -> 0; matrix products, arithmetic and copies ran while one was open for 5% -> 0% of each run, Pallas kernels for 0% -> 0%
where the time goes in v1:
time: 110 us; the launch traced here: 108 us
  Pallas kernels  91.3 us (83%)
  local copies, waits for them, and re-layouts  12.6 us (11%)
  matrix products  3.56 us (3%)
    pallas_call x1, Pallas kernels, on_device(): pl.pallas_call(kernel, out_shape=[S((2, NY, G, H), BF), S((112, R), F32),...  91.3 us
    unnamed x40, local copies, waits for them, and re-layouts  11.7 us

profile of v1, /device:TPU:7, one launch (start us, length us, event | category | flops | bytes accessed | tf_op | source)
XLA Modules:
  0.0 108.5 jit_solution(1442207903271342536)
XLA Ops:
  0.6 0.0 copy-start.9
  0.6 0.0 copy-start.7
  0.7 0.0 copy-start.6
  0.7 0.0 copy-start.10
  0.7 0.0 copy-start.8
  0.7 0.0 copy-start.13
  0.7 0.0 copy-start.12
  0.7 0.0 copy-start.11
  0.7 1.7 %convolution_convert_fusion = bf16[2,64]{1,0:T(2,128)(2,1)S(1)} fusion(bf16[2,7168]{1,0:T(2,128)(2,1)} %param.15, bf16[64,7168]{1,0:T(8,128)(2,1)} %dl_hbm.1), kind=kOutput, calls=%fused_computation | convolution fusion | flops 1835136 | bytes 946432 | tf_op jit(solution)/shard_map/dot_general | solution.py:22
  2.4 1.6 %convolution_convert_fusion.2 = bf16[2,64]{1,0:T(2,128)(2,1)S(1)} fusion(bf16[2,7168]{1,0:T(2,128)(2,1)} %param.14, bf16[7168,64]{0,1:T(8,128)(2,1)} %param.22), kind=kOutput, calls=%fused_computation.2 | convolution fusion | flops 1835136 | bytes 946432 | tf_op jit(solution)/shard_map/dot_general | solution.py:18
  3.9 0.0 copy-done.9
  3.9 0.0 copy-done.7
  3.9 0.4 convolution_convert_fusion.1
  4.3 0.1 maximum_bitcast_fusion.1
  4.4 0.0 copy-done.11
  4.4 0.1 copy.25
  4.5 0.0 copy-done.12
  4.5 0.1 copy.26
  4.6 0.0 copy-done.13
  4.6 0.1 copy.24
  4.7 0.1 maximum_convert_fusion.sc_ref
  4.8 0.0 copy-done.10
  4.8 0.1 maximum_bitcast_fusion
  5.0 0.0 copy-done.8
  5.0 0.1 copy.27.de_ref
  5.1 0.0 copy-done.6
  5.1 1.0 copy.28.ge_hbm
  6.1 0.0 copy-start
  6.1 0.0 copy-start.4
  6.1 0.0 copy-start.5
  6.1 2.7 %copy.29.ue_hbm = bf16[7168,64]{1,0:T(8,128)(2,1)} copy(bf16[7168,64]{0,1:T(8,128)(2,1)} %param.24) | data formatting | bytes 1835008 | tf_op args[10]
  8.9 0.0 copy-done
  8.9 0.0 copy-done.4
  8.9 0.0 copy-done.5
  8.9 0.0 copy-start.1
  8.9 1.2 %copy-done.1 = bf16[1792,256]{1,0:T(8,128)(2,1)S(1)} copy-done((bf16[1792,256]{1,0:T(8,128)(2,1)S(1)}, bf16[1792,256]{1,0:T(8,128)(2,1)}, u32[]{:S(2)}) %copy-start.1) | copy-done | bytes 917528
  10.1 0.0 copy-start.2
  10.1 1.2 %copy-done.2 = bf16[1792,256]{1,0:T(8,128)(2,1)S(1)} copy-done((bf16[1792,256]{1,0:T(8,128)(2,1)S(1)}, bf16[1792,256]{1,0:T(8,128)(2,1)}, u32[]{:S(2)}) %copy-start.2) | copy-done | bytes 917528
  11.2 0.0 copy-start.3
  11.2 1.2 %copy-done.3 = bf16[256,1792]{1,0:T(8,128)(2,1)S(1)} copy-done((bf16[256,1792]{1,0:T(8,128)(2,1)S(1)}, bf16[256,1792]{1,0:T(8,128)(2,1)}, u32[]{:S(2)}) %copy-start.3) | copy-done | bytes 917528
  12.4 91.3 %lora_ffn_step.1 = (bf16[2,4,16,256]{3,2,1,0:T(8,128)(2,1)S(1)}, f32[112,64]{1,0:T(8,128)S(1)}, f32[112,64]{1,0:T(8,128)S(1)}, f32[112,128]{1,0:T(8,128)S(1)}, f...) custom-call(bf16[2,4,16,256]{3,2,1,0:T(8,128)(2,1)S(1)} %reshape.33.send_ref, ...), custom_call_target="tpu_custom_call" | custom-call | tf_op jit(solution)/shard_map/lora_ffn_step/pallas_call | solution.py:605
  103.8 0.7 fusion
  104.4 0.7 copy.32
  105.1 0.7 copy.33
  105.8 0.7 copy.35
  106.5 0.7 copy.34
  107.2 0.6 copy.38
  107.9 0.6 copy.39
  (8 shorter events, 0.2 us)
Async XLA Ops:
  0.6 3.3 %copy-start.9 = (bf16[2,7168]{1,0:T(2,128)(2,1)S(1)}, bf16[2,7168]{1,0:T(2,128)(2,1)}, u32[]{:S(2)}) copy-start(bf16[2,7168]{1,0:T(2,128)(2,1)} %param.14) | copy-start | bytes 86020
  0.6 3.3 %copy-start.7 = (bf16[7168,64]{0,1:T(8,128)(2,1)S(1)}, bf16[7168,64]{0,1:T(8,128)(2,1)}, u32[]{:S(2)}) copy-start(bf16[7168,64]{0,1:T(8,128)(2,1)} %param.24) | copy-start | bytes 2752516
  0.7 4.5 %copy-start.6 = (bf16[7168,64]{0,1:T(8,128)(2,1)S(1)}, bf16[7168,64]{0,1:T(8,128)(2,1)}, u32[]{:S(2)}) copy-start(bf16[7168,64]{0,1:T(8,128)(2,1)} %param.22) | copy-start | bytes 2752516
  0.7 4.2 %copy-start.10 = (bf16[2,7168]{1,0:T(2,128)(2,1)S(1)}, bf16[2,7168]{1,0:T(2,128)(2,1)}, u32[]{:S(2)}) copy-start(bf16[2,7168]{1,0:T(2,128)(2,1)} %param.15) | copy-start | bytes 86020
  0.7 4.3 %copy-start.8 = (bf16[256,64]{0,1:T(8,128)(2,1)S(1)}, bf16[256,64]{0,1:T(8,128)(2,1)}, u32[]{:S(2)}) copy-start(bf16[256,64]{0,1:T(8,128)(2,1)} %param.26) | copy-start | bytes 98308
  0.7 3.9 %copy-start.13 = (bf16[2,14]{1,0:T(2,128)(2,1)S(1)}, bf16[2,14]{1,0:T(2,128)(2,1)}, u32[]{:S(2)}) copy-start(bf16[2,14]{1,0:T(2,128)(2,1)} %param.21) | copy-start | bytes 172
  0.7 3.8 %copy-start.12 = (bf16[14,2]{0,1:T(2,128)(2,1)S(1)}, bf16[14,2]{0,1:T(2,128)(2,1)}, u32[]{:S(2)}) copy-start(bf16[14,2]{0,1:T(2,128)(2,1)} %param.19) | copy-start | bytes 172
  0.7 3.7 %copy-start.11 = (bf16[14,2]{0,1:T(2,128)(2,1)S(1)}, bf16[14,2]{0,1:T(2,128)(2,1)}, u32[]{:S(2)}) copy-start(bf16[14,2]{0,1:T(2,128)(2,1)} %param.17) | copy-start | bytes 172
  6.1 2.8 %copy-start = (bf16[64,7168]{1,0:T(8,128)(2,1)S(1)}, bf16[64,7168]{1,0:T(8,128)(2,1)}, u32[]{:S(2)}) copy-start(bf16[64,7168]{1,0:T(8,128)(2,1)} %dl_hbm.1) | copy-start | bytes 2752516
  6.1 2.8 %copy-start.4 = (bf16[64,256]{1,0:T(8,128)(2,1)S(1)}, bf16[64,256]{1,0:T(8,128)(2,1)}, u32[]{:S(2)}) copy-start(bf16[64,256]{1,0:T(8,128)(2,1)} %gl_ref.1) | copy-start | bytes 98308
  6.1 2.7 %copy-start.5 = (bf16[64,256]{1,0:T(8,128)(2,1)S(1)}, bf16[64,256]{1,0:T(8,128)(2,1)}, u32[]{:S(2)}) copy-start(bf16[64,256]{1,0:T(8,128)(2,1)} %ul_ref.1) | copy-start | bytes 98308
  8.9 1.2 %copy-start.1 = (bf16[1792,256]{1,0:T(8,128)(2,1)S(1)}, bf16[1792,256]{1,0:T(8,128)(2,1)}, u32[]{:S(2)}) copy-start(bf16[1792,256]{1,0:T(8,128)(2,1)} %gc_hbm.1) | copy-start | bytes 2752516
  10.1 1.2 %copy-start.2 = (bf16[1792,256]{1,0:T(8,128)(2,1)S(1)}, bf16[1792,256]{1,0:T(8,128)(2,1)}, u32[]{:S(2)}) copy-start(bf16[1792,256]{1,0:T(8,128)(2,1)} %uc_hbm.1) | copy-start | bytes 2752516
  11.2 1.2 %copy-start.3 = (bf16[256,1792]{1,0:T(8,128)(2,1)S(1)}, bf16[256,1792]{1,0:T(8,128)(2,1)}, u32[]{:S(2)}) copy-start(bf16[256,1792]{1,0:T(8,128)(2,1)} %dc_hbm.1) | copy-start | bytes 2752516

commit v2 on v1

v2 whole, which is shorter than its diff:
```python
import jax
import jax.numpy as jnp
from jax import lax
from jax.experimental import pallas as pl
from jax.experimental.pallas import tpu as pltpu
from jax.sharding import PartitionSpec as P

NX, NZ, NY = 4, 8, 4
KP, KE, EX = 1792, 1920, 128
G, H, R = 16, 256, 64
NB = 384
BF, F32 = jnp.bfloat16, jnp.float32
MESH = pl.DeviceIdType.MESH
ORDER = (0, 7, 1, 6, 2, 5, 3, 4)


def mm(a, b):
    return jnp.dot(a, b, preferred_element_type=F32)


def mm_nt(a, b):
    return lax.dot_general(a, b, (((1,), (1,)), ((), ())), preferred_element_type=F32)


def mm_tn(a, b):
    return lax.dot_general(a, b, (((0,), (0,)), ((), ())), preferred_element_type=F32)


def kernel(
    tok_ref, gout_ref, sc_ref, gc_hbm, uc_hbm, dc_hbm, gl_ref, ul_ref, det_ref, get_hbm, uet_hbm, dl_hbm,
    rows_out, fd_out, dla_out,
    gcv, ucv, dcv, gev, dlv, ldsem,
    sf, sends, st1, s1r,
    wgu, wd, wsr,
    aa, agr,
    ext, extp, exr,
    part, rgu, gur,
    parth, rh, hr,
    hb, hall, hallr,
    gb, gall, gallr,
    po, pq, rss, rsr, rsrs,
    xs, xr, xrs,
    msg, rowsr, rowss,
    sp, sa, sar, sb, sc8, sc8r, sd, se, ser, smm, smr,
    res, mb, fd, t3r,
    dlp, dlr, lar,
    pool_all, pool_core, pool_xy,
):
    f = lax.axis_index("fsdp")
    y = lax.axis_index("dp")
    x = lax.div(f, 16)
    z = lax.rem(lax.div(f, 2), 8)
    c = lax.rem(f, 2)
    o = 1 - c

    def fid(xx, zz, cc):
        return xx * 16 + zz * 2 + cc

    def m4(v):
        return lax.rem(v, 4)

    def m8(v):
        return lax.rem(v, 8)

    zp = [m8(z + k) for k in range(NZ)]
    xp = [m4(x + k) for k in range(NX)]
    yp = [m4(y + k) for k in range(NY)]

    def rcopy(src, dst, ssem, rsem, ff, yy):
        return pltpu.make_async_remote_copy(
            src_ref=src, dst_ref=dst, send_sem=ssem, recv_sem=rsem,
            device_id={"fsdp": ff, "dp": yy}, device_id_type=MESH,
        )

    def wait(ref, sem):
        pltpu.make_async_copy(ref, ref, sem).wait()

    scopes = {
        "all": (pool_all, [], None),
        0: (pool_core, [], lambda: c == 0),
        1: (pool_core, [], lambda: c == 1),
        "xy0": (pool_xy, [], lambda: jnp.logical_and(c == 0, x == y)),
        "xy1": (pool_xy, [], lambda: jnp.logical_and(c == 1, x == y)),
    }
    scope = ["all"]

    def within(name, cond, fn):
        scope.append(name)
        pl.when(cond)(fn)
        scope.pop()

    def send(src, dst, rsem, ff, yy, own=None):
        pool, pending, _ = scopes[scope[-1]]
        ssem = pool.at[len(pending)]
        pending.append((src.shape, own))
        if own is None:
            rcopy(src, dst, ssem, rsem, ff, yy).start()
            return

        @pl.when(own())
        def _():
            pltpu.make_async_copy(src, dst, rsem).start()

        @pl.when(jnp.logical_not(own()))
        def _():
            rcopy(src, dst, ssem, rsem, ff, yy).start()

    def drain(name, now=False):
        pool, pending, cond = scopes[name]

        def body():
            like = {
                (G, H): sp.at[0], (KE, H): wgu.at[0], (H, KE): wd.at[0], (G, KE): aa.at[0, 0],
                (NZ, NX, G, EX): ext, (4, G, H): part.at[0, 0], (2, G, H): parth.at[0, 0],
                (4, G, EX): smm.at[0], (EX, EX): mb.at[0], (R, H): dlp.at[0],
            }
            for i, (shape, own) in enumerate(pending):
                if own is None:
                    wait(like[shape], pool.at[i])
                else:
                    @pl.when(jnp.logical_not(own()))
                    def _(shape=shape, i=i):
                        wait(like[shape], pool.at[i])

        if cond is None or now:
            body()
            pending.clear()
        else:
            pl.when(cond())(body)

    loads = [
        pltpu.make_async_copy(get_hbm, gev.at[pl.ds(0, R)], ldsem.at[0]),
        pltpu.make_async_copy(uet_hbm, gev.at[pl.ds(R, R)], ldsem.at[1]),
        pltpu.make_async_copy(dl_hbm, dlv.at[pl.ds(0, R)], ldsem.at[2]),
        pltpu.make_async_copy(gc_hbm, gcv, ldsem.at[3]),
        pltpu.make_async_copy(uc_hbm, ucv, ldsem.at[4]),
        pltpu.make_async_copy(dc_hbm, dcv, ldsem.at[5]),
    ]
    for ld in loads:
        ld.start()

    barrier = pltpu.get_barrier_semaphore()
    peers = []
    for dy in range(NY):
        for dc in range(2):
            if dy or dc:
                peers.append((fid(x, z, lax.rem(c + dc, 2)), yp[dy]))
    for dx in range(1, NX):
        peers.append((fid(xp[dx], z, c), y))
    for dz in range(1, NZ):
        peers.append((fid(x, zp[dz], c), y))
    for ff, yy in peers:
        pl.semaphore_signal(barrier, inc=1, device_id={"fsdp": ff, "dp": yy}, device_id_type=MESH)

    dlv[R:EX, :] = jnp.zeros((R, NY * KP), BF)
    for kind, ref in enumerate((tok_ref, gout_ref)):
        v = ref[...].astype(F32)
        v16 = jnp.concatenate([v, jnp.zeros((14, NY * KP), F32)], axis=0).astype(BF)
        for yy in range(NY):
            for t in range(2):
                for j in range(7):
                    sf[kind, yy, t * 8 + j : t * 8 + j + 1, :] = v[
                        t : t + 1, yy * KP + j * 256 : yy * KP + (j + 1) * 256
                    ]
        if kind == 0:
            loads[0].wait()
            loads[1].wait()
            e = mm_nt(v16, gev[...])
        else:
            loads[2].wait()
            e = mm_nt(v16, dlv[...])
        for yy in range(NY):
            for t in range(2):
                sf[kind, yy, t * 8 + 7 : t * 8 + 8, :] = jnp.concatenate(
                    [e[t : t + 1], jnp.zeros((1, EX), F32)], axis=1
                )
    sends[...] = sf[...].astype(BF)
    pl.semaphore_wait(barrier, len(peers))

    for dy in (2, 1, 3, 0):
        for kind in range(2):
            send(
                sends.at[kind, yp[dy]], st1.at[y * 2 + c], s1r.at[y * 2 + c],
                fid(x, z, kind), yp[dy], own=(lambda kind=kind: c == kind) if dy == 0 else None,
            )

    def dequant_cols(codes, slot, s0):
        def body(i, carry):
            rows = pl.ds(pl.multiple_of(i * 128, 128), 128)
            wgu[slot, rows, 0:128] = (codes[rows, 0:128].astype(F32) * sc_ref[s0, i]).astype(BF)
            wgu[slot, rows, 128:256] = (codes[rows, 128:256].astype(F32) * sc_ref[s0 + 1, i]).astype(BF)
            return carry

        lax.fori_loop(0, 14, body, 0)

    sib = fid(x, z, o)
    loads[3].wait()
    dequant_cols(gcv, c, 0)
    wgu[c, KP : KP + R, :] = gl_ref[...]
    wgu[c, KP + R :, :] = jnp.zeros((R, H), BF)
    send(wgu.at[c], wgu.at[c], wsr.at[0], sib, y)
    loads[4].wait()
    dequant_cols(ucv, 2 + c, 2)
    wgu[2 + c, KP : KP + R, :] = jnp.zeros((R, H), BF)
    wgu[2 + c, KP + R :, :] = ul_ref[...]
    send(wgu.at[2 + c], wgu.at[2 + c], wsr.at[1], sib, y)
    loads[5].wait()

    def dequant_down(i, carry):
        cols = pl.ds(pl.multiple_of(i * 128, 128), 128)
        wd[c, 0:128, cols] = (dcv[0:128, cols].astype(F32) * sc_ref[4, i]).astype(BF)
        wd[c, 128:256, cols] = (dcv[128:256, cols].astype(F32) * sc_ref[5, i]).astype(BF)
        return carry

    lax.fori_loop(0, 14, dequant_down, 0)
    det = jnp.concatenate([det_ref[...].astype(F32), jnp.zeros((R, H), F32)], axis=0)
    wd[c, :, KP:KE] = det.T.astype(BF)
    send(wd.at[c], wd.at[c], wsr.at[2], sib, y)

    for i in range(8):
        wait(st1.at[i], s1r.at[i])
    got = st1[...].reshape(128, H)
    row8 = lax.broadcasted_iota(jnp.int32, (G, 128), 0) * 8
    col = lax.broadcasted_iota(jnp.int32, (G, 128), 1)
    for j in range(8):
        pick = (col == row8 + j).astype(F32).astype(BF)
        v = mm(pick, got).astype(BF)
        if j < 7:
            aa[z, x, :, j * 256 : (j + 1) * 256] = v
        else:
            aa[z, x, :, KP:KE] = v[:, :EX]

    flag = jnp.where(y == 0, 1.0, 0.0).astype(F32)

    def masked(v):
        return (v.astype(F32) * flag).astype(BF)

    def have(zz, xx):
        wait(aa.at[zz, xx], agr.at[zz * 4 + xx])

    def fwd(zz, xx, tz, tx):
        send(aa.at[zz, xx], aa.at[zz, xx], agr.at[zz * 4 + xx], fid(tx, tz, c), y)

    zr, zl, zf = zp[1], zp[7], zp[4]
    xrt, xlt, xf = xp[1], xp[3], xp[2]

    def weights():
        wait(wgu.at[o], wsr.at[0])
        wait(wgu.at[2 + o], wsr.at[1])
        wait(wd.at[o], wsr.at[2])

    def front0(zs):
        def body(b, carry):
            a = jnp.concatenate([aa[zz].reshape(64, KE) for zz in zs], axis=0)
            acc = mm(a[:, :KP], wgu[b, 0:KP, :]) + mm(masked(a[:, KP:]), wgu[b, KP:KE, :])
            acc = acc.astype(BF)
            for i, zz in enumerate(zs):
                part[zz, :, b] = acc[i * 64 : (i + 1) * 64].reshape(4, G, H)
            return carry

        lax.fori_loop(0, 4, body, 0)
        for zz in zs:
            for xx in range(NX):
                send(
                    part.at[zz, xx], rgu.at[y, m4(zz)], gur.at[y * 4 + m4(zz)],
                    fid(x, z, lax.div(zz, 4)), m4(zz + xx),
                    own=lambda zz=zz, xx=xx: jnp.logical_and(m4(zz + xx) == y, zz < 4),
                )

    def front1(xx):
        def body(b, carry):
            a = aa[:, xx].reshape(128, KE)
            acc = mm_nt(a[:, :KP], wd[b, :, 0:KP]) + mm_nt(masked(a[:, KP:]), wd[b, :, KP:KE])
            parth[xx, :, b] = acc.astype(BF).reshape(8, G, H)
            return carry

        lax.fori_loop(0, 2, body, 0)
        for zz in range(NZ):
            send(
                parth.at[xx, zz], rh.at[y, zz % 4], hr.at[y * 4 + zz % 4],
                fid(x, z, zz // 4), m4(xx + zz),
                own=(lambda xx=xx, zz=zz: m4(xx + zz) == y) if zz >= 4 else None,
            )

    def gather0():
        fwd(z, x, zr, x)
        fwd(z, x, zl, x)
        fwd(z, x, z, xf)
        fwd(z, x, z, xrt)
        fwd(z, x, z, xlt)
        for xx in (xrt, xlt, xf):
            have(z, xx)
            fwd(z, xx, zr, x)
            fwd(z, xx, zl, x)
        weights()
        front0([z])
        for k in range(1, 4):
            za, zb = zp[8 - k], zp[k]
            for i, xx in enumerate((x, xrt, xlt, xf)):
                have(za, xx)
                if k < 3 or i < 2:
                    fwd(za, xx, zr, x)
                have(zb, xx)
                if k < 3 or i >= 2:
                    fwd(zb, xx, zl, x)
            front0([za, zb])
        for xx in range(NX):
            have(zf, xx)
        send(aa.at[:, :, :, pl.ds(KP, EX)], ext, exr, sib, y)
        front0([zf])

    def gather1():
        fwd(z, x, zr, x)
        fwd(z, x, zl, x)

        def spread(zz):
            fwd(zz, x, z, xrt)
            fwd(zz, x, z, xlt)

        def xstep(i):
            zz = zp[ORDER[i]]
            have(zz, xlt)
            if i % 2 == 0:
                fwd(zz, xlt, z, xrt)
            have(zz, xrt)
            if i % 2 == 1:
                fwd(zz, xrt, z, xlt)

        spread(z)
        for k in range(1, 4):
            za, zb = zp[8 - k], zp[k]
            have(za, x)
            fwd(za, x, zr, x)
            spread(za)
            have(zb, x)
            if k < 3:
                fwd(zb, x, zl, x)
            spread(zb)
            for i in {1: (0,), 2: (1, 2), 3: (3, 4)}[k]:
                xstep(i)
        have(zf, x)
        spread(zf)
        weights()
        front1(x)
        for i in (5, 6, 7):
            xstep(i)
        front1(xlt)
        front1(xrt)
        for zz in range(NZ):
            have(zz, xf)
        send(aa.at[:, :, :, pl.ds(KP, EX)], ext, exr, sib, y)
        front1(xf)

    within(0, c == 0, gather0)
    within(1, c == 1, gather1)

    def middle(q, carry):
        for s in range(NY):
            wait(rgu.at[s, q], gur.at[s * 4 + q])
            wait(rh.at[s, q], hr.at[s * 4 + q])
        for b in range(2):
            g = rgu[0, q, b].astype(F32)
            u = rgu[0, q, 2 + b].astype(F32)
            h = rh[0, q, b].astype(F32)
            for s in range(1, NY):
                g += rgu[s, q, b].astype(F32)
                u += rgu[s, q, 2 + b].astype(F32)
                h += rh[s, q, b].astype(F32)
            sig = jax.nn.sigmoid(g)
            act = g * sig
            hb[q, b] = (act * u).astype(BF)
            gb[q, b] = (h * u * sig * (1.0 + g * (1.0 - sig))).astype(BF)
            gb[q, 2 + b] = (h * act).astype(BF)
        return carry

    lax.fori_loop(0, 4, middle, 0)
    blk = c * 4 + y
    for i in range(4):
        qh = m4(z + (0, 3, 1, 2)[i])
        qg = m4(y + 8 - x - (2, 1, 3, 0)[i])
        for dy in (2, 1, 3, 0):
            send(gb.at[qg], gall.at[blk, qg], gallr.at[blk * 4 + qg], fid(x, z, 1), yp[dy],
                 own=(lambda: c == 1) if dy == 0 else None)
            send(hb.at[qh], hall.at[blk, qh], hallr.at[blk * 4 + qh], fid(x, z, 0), yp[dy],
                 own=(lambda: c == 0) if dy == 0 else None)

    def small_a():
        mids = jnp.zeros((64, EX), F32)
        backs = jnp.zeros((64, EX), F32)
        for b in range(2):
            mids += mm(hb[:, b].reshape(64, H), wd[b, :, KP:KE])
        for b in range(4):
            backs += mm_nt(gb[:, b].reshape(64, H), wgu[b, KP:KE, :])
        sp[:, :, 0:EX] = mids.astype(BF).reshape(4, G, EX)
        sp[:, :, EX : 2 * EX] = backs.astype(BF).reshape(4, G, EX)
        for q in range(NX):
            send(sp.at[q], sa.at[x], sar.at[x], fid(q, z, c), y, own=lambda q=q: x == q)

    small_a()

    def small_b():
        for i in range(NX):
            wait(sa.at[i], sar.at[i])
        v = sa[0].astype(F32)
        for i in range(1, NX):
            v += sa[i].astype(F32)
        sb[...] = v.astype(BF)
        for dz in (4, 3, 5, 2, 6, 1, 7):
            send(sb, sc8.at[z], sc8r.at[z], fid(x, zp[dz], c), y)

    def small_c():
        v = sb[...].astype(F32)
        for dz in range(1, NZ):
            wait(sc8.at[zp[dz]], sc8r.at[zp[dz]])
            v += sc8[zp[dz]].astype(F32)
        sd[...] = v.astype(BF)
        for dx in (2, 1, 3):
            send(sd, se.at[x], ser.at[x], fid(xp[dx], z, c), y)

    def small_d():
        for dx in range(1, NX):
            wait(se.at[xp[dx]], ser.at[xp[dx]])
        se[x] = sd[...]
        for cc in range(2):
            lanes = pl.ds((1 - cc) * EX, EX)
            send(se.at[:, :, lanes], smm.at[blk], smr.at[blk], fid(x, z, cc), x,
                 own=lambda cc=cc: jnp.logical_and(c == cc, y == x))

    def small_e():
        for i in range(8):
            wait(smm.at[i], smr.at[i])
        small = jnp.concatenate(
            [smm[(zz // 4) * 4 + (xx + zz) % 4, zz % 4] for zz in range(NZ) for xx in range(NX)], axis=0
        )
        first = lax.div(z * 224, 128) * 128
        lead = z * 224 - first
        win = pl.ds(pl.multiple_of(first, 128), 384)
        res[...] = mm_tn(aa[:, :, :, win].reshape(512, 384), small)
        for cc in range(2):
            mb[cc, 0:112, :] = res[pl.ds(pl.multiple_of(lead + cc * 112, 8), 112), :].astype(BF)
        for dy in (2, 1, 3, 0):
            for cc in range(2):
                send(
                    mb.at[cc], fd.at[c], t3r.at[c], fid(x, z, cc), yp[dy],
                    own=(lambda cc=cc: c == cc) if dy == 0 else None,
                )
        drain(scope[-1], True)

    def order_ext():
        wait(ext, exr)
        for i in range(8):
            for q in range(4):
                zz = (i // 4) * 4 + q
                extp[(i * 4 + q) * G : (i * 4 + q + 1) * G, :] = ext[zz, (i % 4 + 8 - zz) % 4]

    def ring(d, slot, v, tgt):
        rss[d, slot] = v.astype(BF)
        send(rss.at[d, slot], rsr.at[d, slot], rsrs.at[d, slot], tgt, y)

    def come(d, slot):
        wait(rsr.at[d, slot], rsrs.at[d, slot])
        return rsr[d, slot].astype(F32)

    def total(n):
        v = xr[0].astype(F32)
        for i in range(1, n):
            v += xr[i].astype(F32)
        return v

    mycols = pl.ds(pl.multiple_of(y * KP, 128), KP)

    def finish(fin, back):
        mid = fin[:, KP:KE].astype(BF)
        fin = (fin[:, :KP] + mm(mid, back[:, mycols])).astype(BF)
        m = lax.broadcasted_iota(jnp.int32, (128, G), 0)
        r8 = lax.broadcasted_iota(jnp.int32, (128, G), 1) * 8
        acc = jnp.zeros((128, H), F32)
        for j in range(7):
            put = (m == r8 + j).astype(F32).astype(BF)
            acc += mm(put, fin[:, j * 256 : (j + 1) * 256])
        msg[...] = acc.astype(BF).reshape(8, G, H)

    def out0(ts):
        for t in ts:
            for yy in range(NY):
                i = lax.div(t, 4) * 4 + yy
                wait(hall.at[i, m4(t)], hallr.at[i * 4 + m4(t)])

        def rows(kb):
            return jnp.concatenate(
                [hall[lax.div(t, 4) * 4 + m4(t + xx), m4(t), kb] for t in ts for xx in range(NX)], axis=0
            )

        def body(nb, carry):
            cols = pl.ds(pl.multiple_of(nb * NB, 128), NB)
            po[0 : 64 * len(ts), cols] = mm(rows(0), wd[0, :, cols]) + mm(rows(1), wd[1, :, cols])
            return carry

        lax.fori_loop(0, KE // NB, body, 0)

    def scatter0():
        right, left = fid(x, zr, 0), fid(x, zl, 0)
        out0([zf])
        for xx in range(2):
            ring(0, xx, po[xx * G : (xx + 1) * G, :], right)
            ring(1, xx + 2, po[(xx + 2) * G : (xx + 3) * G, :], left)
        small_b()
        for s in range(1, 4):
            out0([zp[4 - s], zp[4 + s]])
            for xx in range(NX):
                v = po[xx * G : (xx + 1) * G, :]
                if s > 1 or xx < 2:
                    v = v + come(0, (s - 1) * 4 + xx)
                ring(0, s * 4 + xx, v, right)
                v = po[(4 + xx) * G : (5 + xx) * G, :]
                if s > 1 or xx >= 2:
                    v = v + come(1, (s - 1) * 4 + xx)
                ring(1, s * 4 + xx, v, left)
            if s == 1:
                small_c()
            if s == 2:
                small_d()
        out0([z])
        within("xy0", x == y, small_e)
        for xx in range(NX):
            v = po[xx * G : (xx + 1) * G, :] + come(0, 12 + xx) + come(1, 12 + xx)
            xs[xx] = v.astype(BF)
            send(xs.at[xx], xr.at[x], xrs.at[x], fid(xx, z, 0), y, own=lambda xx=xx: x == xx)
        order_ext()
        for b in range(2):
            dlp[b] = mm_tn(extp[...], hall[:, :, b].reshape(512, H))[0:R]
        send(dlp.at[1], dlr.at[0], lar.at[0], sib, y)
        for i in range(NX):
            wait(xr.at[i], xrs.at[i])
        finish(total(NX), dlv)

    def out1(t, dst):
        for zz in range(NZ):
            i = (zz // 4) * 4 + m4(t + zz)
            wait(gall.at[i, zz % 4], gallr.at[i * 4 + zz % 4])

        def rows(b):
            return jnp.concatenate(
                [gall[(zz // 4) * 4 + m4(t + zz), zz % 4, b] for zz in range(NZ)], axis=0
            )

        def body(nb, carry):
            cols = pl.ds(pl.multiple_of(nb * NB, 128), NB)
            acc = mm_nt(rows(0), wgu[0, cols, :])
            for b in range(1, 4):
                acc += mm_nt(rows(b), wgu[b, cols, :])
            dst[:, cols] = acc
            return carry

        lax.fori_loop(0, KE // NB, body, 0)

    def scatter1():
        right, left = fid(xrt, z, 1), fid(xlt, z, 1)
        out1(xf, po)
        for zz in range(4):
            ring(0, zz, po[zz * G : (zz + 1) * G, :], right)
            ring(1, zz + 4, po[(zz + 4) * G : (zz + 5) * G, :], left)
        small_b()
        out1(xrt, po)
        for zz in range(4, 8):
            ring(0, 8 + zz, po[zz * G : (zz + 1) * G, :], right)
        out1(xlt, pq)
        for zz in range(4):
            ring(1, 8 + zz, pq[zz * G : (zz + 1) * G, :], left)
        for zz in range(4):
            ring(0, 8 + zz, po[zz * G : (zz + 1) * G, :] + come(0, zz), right)
            ring(1, 12 + zz, pq[(zz + 4) * G : (zz + 5) * G, :] + come(1, zz + 4), left)
        small_c()
        out1(x, po)
        small_d()
        for zz in (4, 5, 6, 7, 0, 1, 2, 3):
            d0, d1 = come(0, 8 + zz), come(1, 8 + zz)
            xs[zz] = (po[zz * G : (zz + 1) * G, :] + d0 + d1).astype(BF)
            send(xs.at[zz], xr.at[z], xrs.at[z], fid(x, zz, 1), y, own=lambda zz=zz: z == zz)
        within("xy1", x == y, small_e)
        order_ext()
        for b in range(4):
            grad = mm_tn(extp[...], gall[:, :, b].reshape(512, H))
            dlp[b] = grad[0:R] if b < 2 else grad[R:EX]
        send(dlp.at[0], dlr.at[0], lar.at[0], sib, y)
        send(dlp.at[2], dlr.at[1], lar.at[1], sib, y)
        for i in range(NZ):
            wait(xr.at[i], xrs.at[i])
        finish(total(NZ), gev)

    within(0, c == 0, scatter0)
    within(1, c == 1, scatter1)

    for dy in (2, 1, 3, 0):
        for cc in range(2):
            send(
                msg.at[yp[dy] * 2 + cc], rowsr.at[c, y], rowss.at[c, y],
                fid(x, z, cc), yp[dy], own=(lambda cc=cc: c == cc) if dy == 0 else None,
            )

    @pl.when(c == 0)
    def _():
        wait(dlr.at[0], lar.at[0])
        wait(dlr.at[1], lar.at[1])
        dla_out[0] = dlp[0]
        dla_out[1] = dlr[0]
        dla_out[2] = dlr[1]

    @pl.when(c == 1)
    def _():
        wait(dlr.at[0], lar.at[0])
        dla_out[0] = dlr[0]
        dla_out[1] = dlp[1]
        dla_out[2] = dlp[3]

    wait(fd.at[0], t3r.at[0])
    wait(fd.at[1], t3r.at[1])
    fd_out[...] = fd[...].astype(F32)
    for k in range(2):
        for s in range(NY):
            wait(rowsr.at[k, s], rowss.at[k, s])
    rows_out[...] = rowsr[...].astype(F32)
    for name in scopes:
        drain(name)


def place(rows_ref, fd_ref, dla_ref, lo, gt, dget, dgl, duet, dul, ddet, ddl, row):
    for kind, ref in enumerate((lo, gt)):
        for yy in range(NY):
            for t in range(2):
                for j in range(7):
                    row[t : t + 1, yy * KP + j * 256 : yy * KP + (j + 1) * 256] = rows_ref[
                        kind, yy, t * 8 + j : t * 8 + j + 1, :
                    ]
        ref[...] = row[...].astype(BF)
    v = fd_ref[0].T
    dget[...] = v[:R, :112]
    duet[...] = v[R:EX, :112]
    ddl[...] = fd_ref[1].T[:R, :112]
    ddet[...] = dla_ref[0]
    dgl[...] = dla_ref[1]
    dul[...] = dla_ref[2]


def dma(*shape):
    return pltpu.SemaphoreType.DMA(shape)


def on_device(
    tokens, grad_out, gate_codes, gate_scales, up_codes, up_scales, down_codes, down_scales,
    gate_enter, gate_leave, up_enter, up_leave, down_enter, down_leave,
):
    scales = jnp.concatenate([gate_scales.T, up_scales.T, down_scales], axis=0).astype(F32)
    vm = pl.BlockSpec(memory_space=pltpu.VMEM)
    sm = pl.BlockSpec(memory_space=pltpu.SMEM)
    hb = pl.BlockSpec(memory_space=pltpu.HBM)
    V = pltpu.VMEM
    one = pltpu.SemaphoreType.DMA
    scratch = [
        V((KP, H), BF), V((KP, H), BF), V((H, KP), BF), V((EX, NY * KP), BF), V((EX, NY * KP), BF), dma(6),
        V((2, NY, G, H), F32), V((2, NY, G, H), BF), V((8, G, H), BF), dma(8),
        V((4, KE, H), BF), V((2, H, KE), BF), dma(3),
        V((NZ, NX, G, KE), BF), dma(32),
        V((NZ, NX, G, EX), BF), V((512, EX), BF), one,
        V((NZ, NX, 4, G, H), BF), V((NY, 4, 4, G, H), BF), dma(16),
        V((NX, NZ, 2, G, H), BF), V((NY, 4, 2, G, H), BF), dma(16),
        V((4, 2, G, H), BF), V((8, 4, 2, G, H), BF), dma(32),
        V((4, 4, G, H), BF), V((8, 4, 4, G, H), BF), dma(32),
        V((128, KE), F32), V((128, KE), F32), V((2, 16, G, KE), BF), V((2, 16, G, KE), BF), dma(2, 16),
        V((8, G, KE), BF), V((8, G, KE), BF), dma(8),
        V((8, G, H), BF), V((2, NY, G, H), BF), dma(2, NY),
        V((4, G, H), BF), V((NX, G, H), BF), dma(NX), V((G, H), BF), V((NZ, G, H), BF), dma(NZ),
        V((G, H), BF), V((NX, G, H), BF), dma(NX), V((8, 4, G, EX), BF), dma(8),
        V((384, EX), F32), V((2, EX, EX), BF), V((2, EX, EX), BF), dma(2),
        V((4, R, H), F32), V((2, R, H), F32), dma(2),
        dma(55), dma(111), dma(8),
    ]
    S = jax.ShapeDtypeStruct
    rows, fd, dla = pl.pallas_call(
        kernel,
        out_shape=[S((2, NY, G, H), F32), S((2, EX, EX), F32), S((3, R, H), F32)],
        in_specs=[vm, vm, sm, hb, hb, hb, vm, vm, vm, hb, hb, hb],
        out_specs=[vm] * 3,
        scratch_shapes=scratch,
        compiler_params=pltpu.CompilerParams(
            collective_id=0, has_side_effects=True, vmem_limit_bytes=63 * 1024 * 1024
        ),
        name="lora_ffn_step",
    )(
        tokens, grad_out, scales, gate_codes, up_codes, down_codes, gate_leave, up_leave, down_enter.T,
        gate_enter.T, up_enter.T, down_leave,
    )
    lo, gt, dget, dgl, duet, dul, ddet, ddl = pl.pallas_call(
        place,
        out_shape=[
            S((2, NY * KP), BF), S((2, NY * KP), BF), S((R, 112), F32), S((R, H), F32),
            S((R, 112), F32), S((R, H), F32), S((R, H), F32), S((R, 112), F32),
        ],
        in_specs=[vm] * 3,
        out_specs=[vm] * 8,
        scratch_shapes=[V((2, NY * KP), F32)],
        name="place_outputs",
    )(rows, fd, dla)
    return lo, gt, dget.T, dgl, duet.T, dul, ddet.T, ddl


def solution(mesh):
    return jax.shard_map(
        on_device,
        mesh=mesh,
        in_specs=(
            P(("fsdp", "dp"), None),
            P(("fsdp", "dp"), None),
            P("dp", "fsdp"),
            P("dp", "fsdp"),
            P("dp", "fsdp"),
            P("dp", "fsdp"),
            P("fsdp", "dp"),
            P("fsdp", "dp"),
            P(),
            P(None, "fsdp"),
            P(),
            P(None, "fsdp"),
            P("fsdp", None),
            P(),
        ),
        out_specs=(
            P(("fsdp", "dp"), None),
            P(("fsdp", "dp"), None),
            P("fsdp", None),
            P(None, "fsdp"),
            P("fsdp", None),
            P(None, "fsdp"),
            P("fsdp", None),
            P(None, "fsdp"),
        ),
        check_vma=False,
    )
```

time: 110 us -> 85 us (0.77); the launches traced: 108 us -> 84.8 us
  local copies, waits for them, and re-layouts: 12.6 us -> 0.66 us
  Pallas kernels: 91.3 us -> 82.8 us
  matrix products: 3.56 us -> 0 us
    unnamed x40 -> x6, local copies, waits for them, and re-layouts: 11.7 us -> 0.66 us
    pallas_call x1 -> x2, Pallas kernels: 91.3 us -> 82.8 us  [the longest x1 81 us: on_device(): pl.pallas_call(kernel, out_shape=[S((2, NY, G, H), F32), S((2, EX, EX), F...]
    dot_general x3 -> x0, matrix products: 3.56 us -> none  [the longest x2 1.91 us: mm(): return jnp.dot(a, b, preferred_element_type=F32)]
where the time goes in v2:
time: 85 us; the launch traced here: 84.8 us
  Pallas kernels  82.8 us (97%)
    pallas_call x1, Pallas kernels, on_device(): pl.pallas_call(kernel, out_shape=[S((2, NY, G, H), F32), S((2, EX, EX), F...  81 us
    pallas_call x1, Pallas kernels, on_device(): pl.pallas_call(place, out_shape=[S((2, NY * KP), BF), S((2, NY * KP), BF)...  1.86 us

profile of v2, /device:TPU:7, one launch (start us, length us, event | category | flops | bytes accessed | tf_op | source)
XLA Modules:
  0.0 84.8 jit_solution(14414309296980156699)
XLA Ops:
  0.6 0.0 copy-start
  0.6 0.0 copy-start.1
  0.7 0.0 copy-start.2
  0.7 0.6 copy-done
  1.3 0.0 copy-done.1
  1.3 0.0 copy-done.2
  1.3 0.6 maximum_convert_fusion.sc_ref
  1.9 81.0 %lora_ffn_step.1 = (f32[2,4,16,256]{3,2,1,0:T(8,128)}, f32[2,128,128]{2,1,0:T(8,128)}, f32[3,64,256]{2,1,0:T(8,128)}) custom-call(bf16[2,7168]{1,0:T(2,128)(2,1)} %tok_ref.1, bf16[2,7168]{1,0:T(2,128)(2,1)} %gout_ref.1, f32[6,14]{1,0:T(8,128)} %maximum_convert_fusion.sc_ref, bf16[1792,256]{1,0:T(8,128)(2,1)} %gc_hbm.1, bf16[1792,256]{1,0:T(8,128)(2,1)} %uc_hbm.1, ...), custom_call_target="tpu_custom_call" | custom-call | tf_op jit(solution)/shard_map/lora_ffn_step/pallas_call | solution.py:679
  82.9 1.9 %place_outputs.1 = (bf16[2,7168]{1,0:T(2,128)(2,1)}, bf16[2,7168]{1,0:T(2,128)(2,1)}, f32[64,112]{1,0:T(8,128)}, f32[64,256]{1,0:T(8,128)}, f32[64,112]{1,0:T(8,...) custom-call(f32[2,4,16,256]{3,2,1,0:T(8,128)} %get-tuple-element.19.rows_ref, ...), custom_call_target="tpu_custom_call" | custom-call | tf_op jit(solution)/shard_map/place_outputs/pallas_call | solution.py:693
Async XLA Ops:
  0.6 0.7 copy-start
  0.6 0.7 copy-start.1
  0.7 0.7 copy-start.2

commit v3 on v2

v3 whole, which is shorter than its diff:
```python
import jax
import jax.numpy as jnp
from jax import lax
from jax.experimental import pallas as pl
from jax.experimental.pallas import tpu as pltpu
from jax.sharding import PartitionSpec as P

NX, NZ, NY = 4, 8, 4
KP, KE, EX = 1792, 1920, 128
G, H, R = 16, 256, 64
NB = 384
BF, F32 = jnp.bfloat16, jnp.float32
MESH = pl.DeviceIdType.MESH


def mm(a, b):
    return jnp.dot(a, b, preferred_element_type=F32)


def mm_nt(a, b):
    return lax.dot_general(a, b, (((1,), (1,)), ((), ())), preferred_element_type=F32)


def mm_tn(a, b):
    return lax.dot_general(a, b, (((0,), (0,)), ((), ())), preferred_element_type=F32)


def kernel(
    tok_hbm, gout_hbm, gs_hbm, us_hbm, ds_hbm, gc_hbm, uc_hbm, dc_hbm, gl_hbm, ul_hbm, det_hbm, get_hbm, uet_hbm, dl_hbm,
    rows_out, fd_out, dla_out,
    tokv, goutv, scv, detv, gcv, ucv, dcv, gev, dlv, ldsem, zsem,
    sf, sends, st1, s1r,
    wgu, wd, wsr,
    aa, agr,
    ext, extp, exr,
    part, rgu, gur,
    parth, rh, hr,
    hb, hall, hallr,
    gb, gall,
    po, pq, rss, rsr, rsrs,
    msg, rows0, rows1, rowss, rowsf, outsem, gota, gotb,
    sp, sa, sar, sb, sc8, sc8r, sd, se, ser, smm, smr,
    res, mb, fd, t3r,
    dlp, dlr, lar,
    gsem,
):
    f = lax.axis_index("fsdp")
    y = lax.axis_index("dp")
    x = lax.div(f, 16)
    z = lax.rem(lax.div(f, 2), 8)
    c = lax.rem(f, 2)
    o = 1 - c

    def fid(xx, zz, cc):
        return xx * 16 + zz * 2 + cc

    def m4(v):
        return lax.rem(v, 4)

    def m8(v):
        return lax.rem(v, 8)

    zp = [m8(z + k) for k in range(NZ)]
    xp = [m4(x + k) for k in range(NX)]
    yp = [m4(y + k) for k in range(NY)]

    def rcopy(src, dst, ssem, rsem, ff, yy):
        return pltpu.make_async_remote_copy(
            src_ref=src, dst_ref=dst, send_sem=ssem, recv_sem=rsem,
            device_id={"fsdp": ff, "dp": yy}, device_id_type=MESH,
        )

    def wait(ref, sem):
        pltpu.make_async_copy(ref, ref, sem).wait()

    def send(src, dst, kind, rsem, ff, yy, own=None):
        ssem = gsem.at[kind]
        if own is None:
            rcopy(src, dst, ssem, rsem, ff, yy).start()
            return

        @pl.when(own)
        def _():
            pltpu.make_async_copy(src, dst, rsem).start()

        @pl.when(jnp.logical_not(own))
        def _():
            rcopy(src, dst, ssem, rsem, ff, yy).start()

    def sent(kind, ref):
        wait(ref, gsem.at[kind])

    loads = [
        pltpu.make_async_copy(get_hbm, gev.at[pl.ds(0, R)], ldsem.at[0]),
        pltpu.make_async_copy(uet_hbm, gev.at[pl.ds(R, R)], ldsem.at[1]),
        pltpu.make_async_copy(dl_hbm, dlv.at[pl.ds(0, R)], ldsem.at[2]),
        pltpu.make_async_copy(gc_hbm, gcv, ldsem.at[3]),
        pltpu.make_async_copy(uc_hbm, ucv, ldsem.at[4]),
        pltpu.make_async_copy(dc_hbm, dcv, ldsem.at[5]),
        pltpu.make_async_copy(tok_hbm, tokv, ldsem.at[6]),
        pltpu.make_async_copy(gout_hbm, goutv, ldsem.at[7]),
        pltpu.make_async_copy(gs_hbm, scv.at[0], ldsem.at[8]),
        pltpu.make_async_copy(gl_hbm, wgu.at[c, pl.ds(KP, R)], ldsem.at[9]),
        pltpu.make_async_copy(ul_hbm, wgu.at[2 + c, pl.ds(KP + R, R)], ldsem.at[10]),
        pltpu.make_async_copy(det_hbm, detv, ldsem.at[11]),
        pltpu.make_async_copy(us_hbm, scv.at[1], ldsem.at[12]),
        pltpu.make_async_copy(ds_hbm, scv.at[2], ldsem.at[13]),
    ]
    for i in (6, 7, 0, 1, 2, 8, 12, 13, 9, 3, 10, 4, 11, 5):
        loads[i].start()

    barrier = pltpu.get_barrier_semaphore()
    peers = []
    for dx in range(NX):
        for dy in range(NY):
            for dc in range(2):
                if dx or dy or dc:
                    peers.append((fid(xp[dx], z, lax.rem(c + dc, 2)), yp[dy]))
    for dz in range(1, NZ):
        peers.append((fid(x, zp[dz], c), y))
    for ff, yy in peers:
        pl.semaphore_signal(barrier, inc=1, device_id={"fsdp": ff, "dp": yy}, device_id_type=MESH)

    dlv[R:EX, :] = jnp.zeros((R, NY * KP), BF)
    for kind, ref in enumerate((tokv, goutv)):
        loads[6 + kind].wait()
        v = ref[...].astype(F32)
        v16 = jnp.concatenate([v, jnp.zeros((14, NY * KP), F32)], axis=0).astype(BF)
        for yy in range(NY):
            for t in range(2):
                for j in range(7):
                    sf[kind, yy, t * 8 + j : t * 8 + j + 1, :] = v[
                        t : t + 1, yy * KP + j * 256 : yy * KP + (j + 1) * 256
                    ]
        if kind == 0:
            loads[0].wait()
            loads[1].wait()
            e = mm_nt(v16, gev[...])
        else:
            loads[2].wait()
            e = mm_nt(v16, dlv[...])
        for yy in range(NY):
            for t in range(2):
                sf[kind, yy, t * 8 + 7 : t * 8 + 8, :] = jnp.concatenate(
                    [e[t : t + 1], jnp.zeros((1, EX), F32)], axis=1
                )
    sends[...] = sf[...].astype(BF)
    pl.semaphore_wait(barrier, len(peers))

    for dz in range(1, NZ):
        pl.semaphore_signal(
            zsem, inc=1, device_id={"fsdp": fid(x, zp[dz], c), "dp": y}, device_id_type=MESH
        )

    src1 = y * 2 + c
    for dx in (2, 1, 3, 0):
        for dy in (2, 1, 3, 0):
            send(
                sends.at[0, yp[dy]], st1.at[x, src1], 0, s1r.at[x], fid(xp[dx], z, 0), yp[dy],
                own=(c == 0) if dx == 0 and dy == 0 else None,
            )
            if dx == 0:
                send(
                    sends.at[1, yp[dy]], st1.at[x, src1], 0, s1r.at[x], fid(x, z, 1), yp[dy],
                    own=(c == 1) if dy == 0 else None,
                )

    def scale(k, i):
        lane = lax.broadcasted_iota(jnp.int32, (2, 14), 1)
        return jnp.sum(jnp.where(lane == i, scv[k].astype(F32), 0.0), axis=1, keepdims=True)

    def dequant_cols(codes, slot, k):
        def body(i, carry):
            rows = pl.ds(pl.multiple_of(i * 128, 128), 128)
            v = scale(k, i)
            wgu[slot, rows, 0:128] = (codes[rows, 0:128].astype(F32) * v[0:1]).astype(BF)
            wgu[slot, rows, 128:256] = (codes[rows, 128:256].astype(F32) * v[1:2]).astype(BF)
            return carry

        lax.fori_loop(0, 14, body, 0)

    sib = fid(x, z, o)
    for i in (8, 12, 13):
        loads[i].wait()
    loads[3].wait()
    dequant_cols(gcv, c, 0)
    loads[9].wait()
    wgu[c, KP + R :, :] = jnp.zeros((R, H), BF)
    send(wgu.at[c], wgu.at[c], 1, wsr.at[0], sib, y)
    loads[4].wait()
    dequant_cols(ucv, 2 + c, 1)
    wgu[2 + c, KP : KP + R, :] = jnp.zeros((R, H), BF)
    loads[10].wait()
    send(wgu.at[2 + c], wgu.at[2 + c], 2, wsr.at[1], sib, y)
    loads[5].wait()
    loads[11].wait()

    def dequant_down(i, carry):
        cols = pl.ds(pl.multiple_of(i * 128, 128), 128)
        v = scale(2, i)
        wd[c, 0:128, cols] = (dcv[0:128, cols].astype(F32) * v[0:1]).astype(BF)
        wd[c, 128:256, cols] = (dcv[128:256, cols].astype(F32) * v[1:2]).astype(BF)
        return carry

    lax.fori_loop(0, 14, dequant_down, 0)
    det = jnp.concatenate([detv[...].astype(F32), jnp.zeros((R, H), F32)], axis=0)
    wd[c, :, KP:KE] = det.T.astype(BF)
    send(wd.at[c], wd.at[c], 3, wsr.at[2], sib, y)

    def unpack(xx):
        wait(st1.at[xx], s1r.at[xx])
        got = st1[xx].reshape(128, H).astype(F32)
        for h, part_ref in enumerate((gota, gotb)):
            part_ref[...] = got[:, h * 128 : (h + 1) * 128]
            for j in range(8 - h):
                k = 2 * j + h
                aa[z, xx, :, k * 128 : (k + 1) * 128] = part_ref[pl.ds(j, G, stride=8), :].astype(BF)

    flag = jnp.where(y == 0, 1.0, 0.0).astype(F32)

    def masked(v):
        return (v.astype(F32) * flag).astype(BF)

    def have(zz, xx):
        wait(aa.at[zz, xx], agr.at[zz * 4 + xx])

    def fwd(zz, xx, tz, tx):
        send(aa.at[zz, xx], aa.at[zz, xx], 4, agr.at[zz * 4 + xx], fid(tx, tz, c), y)

    zr, zl, zf = zp[1], zp[7], zp[4]
    xrt, xlt, xf = xp[1], xp[3], xp[2]

    def weights():
        wait(wgu.at[o], wsr.at[0])
        wait(wgu.at[2 + o], wsr.at[1])
        wait(wd.at[o], wsr.at[2])

    def front0(zs):
        def body(b, carry):
            a = jnp.concatenate([aa[zz].reshape(64, KE) for zz in zs], axis=0)
            acc = mm(a[:, :KP], wgu[b, 0:KP, :]) + mm(masked(a[:, KP:]), wgu[b, KP:KE, :])
            acc = acc.astype(BF)
            for i, zz in enumerate(zs):
                part[zz, :, b] = acc[i * 64 : (i + 1) * 64].reshape(4, G, H)
            return carry

        lax.fori_loop(0, 4, body, 0)
        for zz in zs:
            for xx in range(NX):
                send(
                    part.at[zz, xx], rgu.at[y, m4(zz)], 6, gur.at[m4(zz)],
                    fid(x, z, lax.div(zz, 4)), m4(zz + xx),
                    own=jnp.logical_and(m4(zz + xx) == y, zz < 4),
                )

    def front1(xx):
        def body(b, carry):
            a = aa[:, xx].reshape(128, KE)
            acc = mm_nt(a[:, :KP], wd[b, :, 0:KP]) + mm_nt(masked(a[:, KP:]), wd[b, :, KP:KE])
            parth[xx, :, b] = acc.astype(BF).reshape(8, G, H)
            return carry

        lax.fori_loop(0, 2, body, 0)
        for zz in range(NZ):
            send(
                parth.at[xx, zz], rh.at[y, zz % 4], 6, hr.at[zz % 4],
                fid(x, z, zz // 4), m4(xx + zz), own=(m4(xx + zz) == y) if zz >= 4 else None,
            )

    def gather0():
        for xx in (x, xrt, xlt, xf):
            unpack(xx)
            fwd(z, xx, zr, x)
            fwd(z, xx, zl, x)
        weights()
        front0([z])
        for k in range(1, 4):
            za, zb = zp[8 - k], zp[k]
            for i, xx in enumerate((x, xrt, xlt, xf)):
                have(za, xx)
                if k < 3 or i < 1:
                    fwd(za, xx, zr, x)
                have(zb, xx)
                if k < 3 or i >= 1:
                    fwd(zb, xx, zl, x)
            front0([za, zb])
        for xx in range(NX):
            have(zf, xx)
        send(aa.at[:, :, :, pl.ds(KP, EX)], ext, 5, exr, sib, y)
        front0([zf])

    def gather1():
        unpack(x)
        for dz in (1, 7, 2, 6):
            fwd(z, x, zp[dz], x)

        def spread(zz, far=False):
            fwd(zz, x, z, xrt)
            fwd(zz, x, z, xlt)
            if far:
                fwd(zz, x, z, xf)

        def xstep(dz):
            have(zp[dz], xrt)
            fwd(zp[dz], xrt, z, xlt)

        spread(z)
        have(zp[7], x)
        spread(zp[7])
        have(zp[1], x)
        spread(zp[1])
        have(zp[6], x)
        fwd(zp[6], x, zr, x)
        fwd(zp[6], x, zp[2], x)
        have(zp[2], x)
        fwd(zp[2], x, zl, x)
        spread(zp[6])
        spread(zp[2])
        xstep(0)
        xstep(7)
        xstep(1)
        for dz in (5, 3, 4):
            have(zp[dz], x)
            spread(zp[dz], True)
        xstep(6)
        xstep(2)
        weights()
        front1(x)
        for dz in (3, 4, 5):
            have(zp[dz], xrt)
        front1(xrt)
        for dz in range(NZ):
            have(zp[dz], xlt)
        front1(xlt)
        for dz in range(NZ):
            have(zp[dz], xf)
        send(aa.at[:, :, :, pl.ds(KP, EX)], ext, 5, exr, sib, y)
        front1(xf)

    pl.when(c == 0)(gather0)
    pl.when(c == 1)(gather1)

    def middle(q, carry):
        wait(rgu.at[:, q], gur.at[q])
        wait(rh.at[:, q], hr.at[q])
        for b in range(2):
            g = rgu[0, q, b].astype(F32)
            u = rgu[0, q, 2 + b].astype(F32)
            h = rh[0, q, b].astype(F32)
            for s in range(1, NY):
                g += rgu[s, q, b].astype(F32)
                u += rgu[s, q, 2 + b].astype(F32)
                h += rh[s, q, b].astype(F32)
            sig = jax.nn.sigmoid(g)
            act = g * sig
            hb[q, b] = (act * u).astype(BF)
            gb[q, b] = (h * u * sig * (1.0 + g * (1.0 - sig))).astype(BF)
            gb[q, 2 + b] = (h * act).astype(BF)
        return carry

    lax.fori_loop(0, 4, middle, 0)
    blk = c * 4 + y
    for i in range(4):
        qh = m4(z + (0, 3, 1, 2)[i])
        qg = m4(y + 8 - x - (2, 1, 3, 0)[i])
        for dy in (2, 1, 3, 0):
            send(gb.at[qg], gall.at[blk, qg], 7, hallr.at[m4(y + 4 - qg)], fid(x, z, 1), yp[dy],
                 own=(c == 1) if dy == 0 else None)
            send(hb.at[qh], hall.at[blk, qh], 8, hallr.at[c * 4 + qh], fid(x, z, 0), yp[dy],
                 own=(c == 0) if dy == 0 else None)

    def small_a():
        mids = jnp.zeros((64, EX), F32)
        backs = jnp.zeros((64, EX), F32)
        for b in range(2):
            mids += mm(hb[:, b].reshape(64, H), wd[b, :, KP:KE])
        for b in range(4):
            backs += mm_nt(gb[:, b].reshape(64, H), wgu[b, KP:KE, :])
        sp[:, :, 0:EX] = mids.astype(BF).reshape(4, G, EX)
        sp[:, :, EX : 2 * EX] = backs.astype(BF).reshape(4, G, EX)
        for q in range(NX):
            send(sp.at[q], sa.at[x], 9, sar, fid(q, z, c), y, own=x == q)

    def small_b():
        wait(sa, sar)
        v = sa[0].astype(F32)
        for i in range(1, NX):
            v += sa[i].astype(F32)
        sb[...] = v.astype(BF)
        for dz in (4, 3, 5, 2, 6, 1, 7):
            send(sb, sc8.at[z], 10, sc8r, fid(x, zp[dz], c), y)

    def small_c():
        v = sb[...].astype(F32)
        wait(sc8.at[pl.ds(0, NZ - 1)], sc8r)
        for dz in range(1, NZ):
            v += sc8[zp[dz]].astype(F32)
        sd[...] = v.astype(BF)
        for dx in (2, 1, 3):
            send(sd, se.at[x], 11, ser, fid(xp[dx], z, c), y)

    def small_d():
        wait(se.at[pl.ds(0, NX - 1)], ser)
        se[x] = sd[...]
        for cc in range(2):
            lanes = pl.ds((1 - cc) * EX, EX)
            send(se.at[:, :, lanes], smm.at[blk], 12 + cc, smr, fid(x, z, cc), x,
                 own=jnp.logical_and(c == cc, y == x))

    def small_e():
        wait(smm, smr)
        small = jnp.concatenate(
            [smm[(zz // 4) * 4 + (xx + zz) % 4, zz % 4] for zz in range(NZ) for xx in range(NX)], axis=0
        )
        first = lax.div(z * 224, 128) * 128
        lead = z * 224 - first
        win = pl.ds(pl.multiple_of(first, 128), 384)
        res[...] = mm_tn(aa[:, :, :, win].reshape(512, 384), small)
        for cc in range(2):
            mb[cc, 0:112, :] = res[pl.ds(pl.multiple_of(lead + cc * 112, 8), 112), :].astype(BF)
        for dy in (2, 1, 3, 0):
            for cc in range(2):
                send(
                    mb.at[cc], fd.at[c], 17, t3r.at[c], fid(x, z, cc), yp[dy],
                    own=(c == cc) if dy == 0 else None,
                )
        sent(17, part.at[pl.ds(0, 7), 0])

    def order_ext():
        wait(ext, exr)
        for i in range(8):
            for q in range(4):
                zz = (i // 4) * 4 + q
                extp[(i * 4 + q) * G : (i * 4 + q + 1) * G, :] = ext[zz, (i % 4 + 8 - zz) % 4]

    def ring(d, slot, v, tgt):
        k = d * 16 + slot
        rss[k] = v.astype(BF)
        send(rss.at[k], rsr.at[k], 14, rsrs.at[k], tgt, y)

    def come(d, slot):
        k = d * 16 + slot
        wait(rsr.at[k], rsrs.at[k])
        return rsr[k].astype(F32)

    mycols = pl.ds(pl.multiple_of(y * KP, 128), KP)

    def last(g, v, back, xx, zz, here, rows, rsem, slot):
        v = v[:, :KP] + mm(v[:, KP:KE].astype(BF), back[:, mycols])
        for j in range(7):
            gota[pl.ds(j, G, stride=8), :] = v[:, j * 256 : j * 256 + 128]
            gotb[pl.ds(j, G, stride=8), :] = v[:, j * 256 + 128 : (j + 1) * 256]
        msg[g * 8 : (g + 1) * 8, :, 0:128] = gota[...].astype(BF).reshape(8, G, 128)
        msg[g * 8 : (g + 1) * 8, :, 128:256] = gotb[...].astype(BF).reshape(8, G, 128)
        for dy in (2, 1, 3, 0):
            for cc in range(2):
                send(
                    msg.at[g * 8 + yp[dy] * 2 + cc], rows.at[slot, y], 16, rsem, fid(xx, zz, cc), yp[dy],
                    own=jnp.logical_and(c == cc, here) if dy == 0 else None,
                )

    def out0(ts):
        for t in ts:
            wait(hall.at[pl.ds(lax.div(t, 4) * 4, 4), m4(t)], hallr.at[t])

        def rows(kb):
            return jnp.concatenate(
                [hall[lax.div(t, 4) * 4 + m4(t + xx), m4(t), kb] for t in ts for xx in range(NX)], axis=0
            )

        def body(nb, carry):
            cols = pl.ds(pl.multiple_of(nb * NB, 128), NB)
            po[0 : 64 * len(ts), cols] = mm(rows(0), wd[0, :, cols]) + mm(rows(1), wd[1, :, cols])
            return carry

        lax.fori_loop(0, KE // NB, body, 0)

    def scatter0():
        right, left = fid(x, zr, 0), fid(x, zl, 0)
        out0([zf])
        for xx in range(2):
            ring(0, xx, po[xx * G : (xx + 1) * G, :], right)
            ring(1, xx + 2, po[(xx + 2) * G : (xx + 3) * G, :], left)
        small_a()
        pl.semaphore_wait(zsem, NZ - 1)
        for s in range(1, 4):
            out0([zp[4 - s], zp[4 + s]])
            for xx in range(NX):
                v = po[xx * G : (xx + 1) * G, :]
                if s > 1 or xx < 2:
                    v = v + come(0, (s - 1) * 4 + xx)
                ring(0, s * 4 + xx, v, right)
                v = po[(4 + xx) * G : (5 + xx) * G, :]
                if s > 1 or xx >= 2:
                    v = v + come(1, (s - 1) * 4 + xx)
                ring(1, s * 4 + xx, v, left)
            (small_b, small_c, small_d)[s - 1]()
        out0([z])
        for xx in range(NX):
            v = po[xx * G : (xx + 1) * G, :] + come(0, 12 + xx) + come(1, 12 + xx)
            last(xx, v, dlv, xx, z, x == xx, rows0, rowss.at[0], x)
        order_ext()
        for b in range(2):
            dlp[b] = mm_tn(extp[...], hall[:, :, b].reshape(512, H))[0:R]
        send(dlp.at[1], dlr.at[0], 15, lar.at[0], sib, y)
        pl.when(x == y)(small_e)
        sent(4, rsr.at[pl.ds(0, 28)])
        sent(6, part.at[pl.ds(0, 7)])
        sent(7, part.at[pl.ds(0, 4)])
        sent(8, part.at[pl.ds(0, 3), pl.ds(0, 2)])
        sent(14, rsr.at[pl.ds(0, 28)])
        sent(15, dlp.at[0])
        sent(16, msg.at[pl.ds(0, 31)])

    def out1(t, dst):
        wait(gall.at[:, 0], hallr.at[t])

        def rows(b):
            return jnp.concatenate(
                [gall[(zz // 4) * 4 + m4(t + zz), zz % 4, b] for zz in range(NZ)], axis=0
            )

        def body(nb, carry):
            cols = pl.ds(pl.multiple_of(nb * NB, 128), NB)
            acc = mm_nt(rows(0), wgu[0, cols, :])
            for b in range(1, 4):
                acc += mm_nt(rows(b), wgu[b, cols, :])
            dst[:, cols] = acc
            return carry

        lax.fori_loop(0, KE // NB, body, 0)

    def scatter1():
        right, left = fid(xrt, z, 1), fid(xlt, z, 1)
        out1(xf, po)
        for zz in range(4):
            ring(0, zz, po[zz * G : (zz + 1) * G, :], right)
            ring(1, zz + 4, po[(zz + 4) * G : (zz + 5) * G, :], left)
        small_a()
        pl.semaphore_wait(zsem, NZ - 1)
        out1(xrt, po)
        for zz in range(4, 8):
            ring(0, 8 + zz, po[zz * G : (zz + 1) * G, :], right)
        out1(xlt, pq)
        for zz in range(4):
            ring(1, 8 + zz, pq[zz * G : (zz + 1) * G, :], left)
        for zz in range(4):
            ring(0, 8 + zz, po[zz * G : (zz + 1) * G, :] + come(0, zz), right)
            ring(1, 12 + zz, pq[(zz + 4) * G : (zz + 5) * G, :] + come(1, zz + 4), left)
        small_b()
        out1(x, po)
        small_c()
        for zz in (0, 4, 1, 5, 2, 6, 3, 7):
            v = po[zz * G : (zz + 1) * G, :] + come(0, 8 + zz) + come(1, 8 + zz)
            last(zz, v, gev, x, zz, z == zz, rows1, rowss.at[1], z)
        small_d()
        order_ext()
        for b in range(4):
            grad = mm_tn(extp[...], gall[:, :, b].reshape(512, H))
            dlp[b] = grad[0:R] if b < 2 else grad[R:EX]
        send(dlp.at[0], dlr.at[0], 15, lar.at[0], sib, y)
        send(dlp.at[2], dlr.at[1], 15, lar.at[1], sib, y)
        pl.when(x == y)(small_e)
        sent(4, rsr.at[pl.ds(0, 31)])
        sent(6, part.at[pl.ds(0, 7), pl.ds(0, 2)])
        sent(7, part.at[pl.ds(0, 3)])
        sent(8, part.at[pl.ds(0, 2)])
        sent(14, rsr.at[pl.ds(0, 24)])
        sent(15, dlp.at[pl.ds(0, 2)])
        sent(16, msg.at[pl.ds(0, 63)])

    pl.when(c == 0)(scatter0)
    pl.when(c == 1)(scatter1)

    def give(pairs):
        for i, (ref, sem) in enumerate(pairs):
            if sem is not None:
                wait(ref, sem)
            pltpu.make_async_copy(ref, dla_out.at[i], outsem.at[i]).start()

    pl.when(c == 0)(lambda: give(((dlp.at[0], None), (dlr.at[0], lar.at[0]), (dlr.at[1], lar.at[1]))))
    pl.when(c == 1)(lambda: give(((dlr.at[0], lar.at[0]), (dlp.at[1], None), (dlp.at[3], None))))
    wait(fd.at[0], t3r.at[0])
    wait(fd.at[1], t3r.at[1])
    out_fd = pltpu.make_async_copy(fd, fd_out, outsem.at[3])
    out_fd.start()
    for kind, (rows, n) in enumerate(((rows0, NX), (rows1, NZ))):
        wait(rows, rowss.at[kind])
        v = rows[0].astype(F32)
        for i in range(1, n):
            v += rows[i].astype(F32)
        rowsf[kind] = v
    out_rows = pltpu.make_async_copy(rowsf, rows_out, outsem.at[4])
    out_rows.start()
    for i in range(3):
        wait(dlp.at[0], outsem.at[i])
    out_fd.wait()
    out_rows.wait()
    sent(0, msg.at[pl.ds(0, 19)])
    sent(1, wgu.at[0])
    sent(2, wgu.at[0])
    sent(3, wd.at[0])
    sent(5, ext)
    sent(9, msg.at[pl.ds(0, 3)])
    sent(10, msg.at[pl.ds(0, 7)])
    sent(11, msg.at[pl.ds(0, 3)])
    for cc in range(2):
        @pl.when(jnp.logical_not(jnp.logical_and(c == cc, y == x)))
        def _(cc=cc):
            sent(12 + cc, smm.at[0])


def place(rows_ref, fd_ref, dla_ref, lo, gt, dget, dgl, duet, dul, ddet, ddl, row):
    for kind, ref in enumerate((lo, gt)):
        for yy in range(NY):
            for t in range(2):
                for j in range(7):
                    row[t : t + 1, yy * KP + j * 256 : yy * KP + (j + 1) * 256] = rows_ref[
                        kind, yy, t * 8 + j : t * 8 + j + 1, :
                    ]
        ref[...] = row[...].astype(BF)
    v = fd_ref[0].astype(F32).T
    dget[...] = v[:R, :112]
    duet[...] = v[R:EX, :112]
    ddl[...] = fd_ref[1].astype(F32).T[:R, :112]
    ddet[...] = dla_ref[0]
    dgl[...] = dla_ref[1]
    dul[...] = dla_ref[2]


def dma(*shape):
    return pltpu.SemaphoreType.DMA(shape)


def on_device(
    tokens, grad_out, gate_codes, gate_scales, up_codes, up_scales, down_codes, down_scales,
    gate_enter, gate_leave, up_enter, up_leave, down_enter, down_leave,
):
    vm = pl.BlockSpec(memory_space=pltpu.VMEM)
    hb = pl.BlockSpec(memory_space=pltpu.HBM)
    V = pltpu.VMEM
    one = pltpu.SemaphoreType.DMA
    scratch = [
        V((2, NY * KP), BF), V((2, NY * KP), BF), V((3, 2, 14), BF), V((R, H), BF),
        V((KP, H), BF), V((KP, H), BF), V((H, KP), BF), V((EX, NY * KP), BF), V((EX, NY * KP), BF), dma(14),
        pltpu.SemaphoreType.REGULAR,
        V((2, NY, G, H), F32), V((2, NY, G, H), BF), V((NX, 8, G, H), BF), dma(NX),
        V((4, KE, H), BF), V((2, H, KE), BF), dma(3),
        V((NZ, NX, G, KE), BF), dma(32),
        V((NZ, NX, G, EX), BF), V((512, EX), BF), one,
        V((NZ, NX, 4, G, H), BF), V((NY, 4, 4, G, H), BF), dma(4),
        V((NX, NZ, 2, G, H), BF), V((NY, 4, 2, G, H), BF), dma(4),
        V((4, 2, G, H), BF), V((8, 4, 2, G, H), BF), dma(8),
        V((4, 4, G, H), BF), V((8, 4, 4, G, H), BF),
        V((128, KE), F32), V((128, KE), F32), V((32, G, KE), BF), V((32, G, KE), BF), dma(32),
        V((64, G, H), BF), V((NX, NY, G, H), BF), V((NZ, NY, G, H), BF), dma(2),
        V((2, NY, G, H), F32), dma(5), V((128, 128), F32), V((128, 128), F32),
        V((4, G, H), BF), V((NX, G, H), BF), one, V((G, H), BF), V((NZ, G, H), BF), one,
        V((G, H), BF), V((NX, G, H), BF), one, V((8, 4, G, EX), BF), one,
        V((384, EX), F32), V((2, EX, EX), BF), V((2, EX, EX), BF), dma(2),
        V((4, R, H), F32), V((2, R, H), F32), dma(2),
        dma(18),
    ]
    S = jax.ShapeDtypeStruct
    rows, fd, dla = pl.pallas_call(
        kernel,
        out_shape=[S((2, NY, G, H), F32), S((2, EX, EX), BF), S((3, R, H), F32)],
        in_specs=[hb] * 14,
        out_specs=[hb] * 3,
        scratch_shapes=scratch,
        compiler_params=pltpu.CompilerParams(
            collective_id=0, has_side_effects=True, vmem_limit_bytes=63 * 1024 * 1024
        ),
        name="lora_ffn_step",
    )(
        tokens, grad_out, gate_scales.T, up_scales.T, down_scales, gate_codes, up_codes, down_codes, gate_leave, up_leave, down_enter.T,
        gate_enter.T, up_enter.T, down_leave,
    )
    lo, gt, dget, dgl, duet, dul, ddet, ddl = pl.pallas_call(
        place,
        out_shape=[
            S((2, NY * KP), BF), S((2, NY * KP), BF), S((R, 112), F32), S((R, H), F32),
            S((R, 112), F32), S((R, H), F32), S((R, H), F32), S((R, 112), F32),
        ],
        in_specs=[vm] * 3,
        out_specs=[vm] * 8,
        scratch_shapes=[V((2, NY * KP), F32)],
        name="place_outputs",
    )(rows, fd, dla)
    return lo, gt, dget.T, dgl, duet.T, dul, ddet.T, ddl


def solution(mesh):
    return jax.shard_map(
        on_device,
        mesh=mesh,
        in_specs=(
            P(("fsdp", "dp"), None),
            P(("fsdp", "dp"), None),
            P("dp", "fsdp"),
            P("dp", "fsdp"),
            P("dp", "fsdp"),
            P("dp", "fsdp"),
            P("fsdp", "dp"),
            P("fsdp", "dp"),
            P(),
            P(None, "fsdp"),
            P(),
            P(None, "fsdp"),
            P("fsdp", None),
            P(),
        ),
        out_specs=(
            P(("fsdp", "dp"), None),
            P(("fsdp", "dp"), None),
            P("fsdp", None),
            P(None, "fsdp"),
            P("fsdp", None),
            P(None, "fsdp"),
            P("fsdp", None),
            P(None, "fsdp"),
        ),
        check_vma=False,
    )
```

time: 85 us -> 76.3 us (0.90)
  Pallas kernels: 82.8 us -> 75 us
    pallas_call x1, Pallas kernels: 81 us -> 73.2 us  [on_device(): pl.pallas_call(kernel, out_shape=[S((2, NY, G, H), F32), S((2, EX, EX), B...]
where the time goes in v3:
time: 76.3 us; the launch traced here: 75.7 us
  Pallas kernels  75 us (98%)
    pallas_call x1, Pallas kernels, on_device(): pl.pallas_call(kernel, out_shape=[S((2, NY, G, H), F32), S((2, EX, EX), B...  73.2 us
    pallas_call x1, Pallas kernels, on_device(): pl.pallas_call(place, out_shape=[S((2, NY * KP), BF), S((2, NY * KP), BF)...  1.83 us

profile of v3, /device:TPU:7, one launch (start us, length us, event | category | flops | bytes accessed | tf_op | source)
XLA Modules:
  0.0 75.7 jit_solution(16903194788055279247)
XLA Ops:
  0.6 73.2 %lora_ffn_step.1 = (f32[2,4,16,256]{3,2,1,0:T(8,128)}, bf16[2,128,128]{2,1,0:T(8,128)(2,1)}, f32[3,64,256]{2,1,0:T(8,128)}) custom-call(bf16[2,7168]{1,0:T(2,128)(2,1)} %tok_hbm.1, bf16[2,7168]{1,0:T(2,128)(2,1)} %gout_hbm.1, bf16[2,14]{1,0:T(2,128)(2,1)} %bitcast.11, bf16[2,14]{1,0:T(2,128)(2,1)} %bitcast.12, bf16[2,14]{1,0:T(2,128)(2,1)} %ds_hbm.1, ...), custom_call_target="tpu_custom_call" | custom-call | tf_op jit(solution)/shard_map/lora_ffn_step/pallas_call | solution.py:665
  73.8 1.8 %place_outputs.1 = (bf16[2,7168]{1,0:T(2,128)(2,1)}, bf16[2,7168]{1,0:T(2,128)(2,1)}, f32[64,112]{1,0:T(8,128)}, f32[64,256]{1,0:T(8,128)}, f32[64,112]{1,0:T(8,...) custom-call(f32[2,4,16,256]{3,2,1,0:T(8,128)} %get-tuple-element.19.rows_ref, ...), custom_call_target="tpu_custom_call" | custom-call | tf_op jit(solution)/shard_map/place_outputs/pallas_call | solution.py:679

commit v4 on v3

--- a/solution.py
+++ b/solution.py
@@ -153,17 +153,17 @@
         )
 
     src1 = y * 2 + c
-    for dx in (2, 1, 3, 0):
+    for dy in (2, 1, 3, 0):
+        send(
+            sends.at[1, yp[dy]], st1.at[x, src1], 0, s1r.at[x], fid(x, z, 1), yp[dy],
+            own=(c == 1) if dy == 0 else None,
+        )
+    for dx in (0, 1, 3, 2):
         for dy in (2, 1, 3, 0):
             send(
                 sends.at[0, yp[dy]], st1.at[x, src1], 0, s1r.at[x], fid(xp[dx], z, 0), yp[dy],
                 own=(c == 0) if dx == 0 and dy == 0 else None,
             )
-            if dx == 0:
-                send(
-                    sends.at[1, yp[dy]], st1.at[x, src1], 0, s1r.at[x], fid(x, z, 1), yp[dy],
-                    own=(c == 1) if dy == 0 else None,
-                )
 
     def scale(k, i):
         lane = lax.broadcasted_iota(jnp.int32, (2, 14), 1)
@@ -300,9 +300,10 @@
             if far:
                 fwd(zz, x, z, xf)
 
-        def xstep(dz):
-            have(zp[dz], xrt)
-            fwd(zp[dz], xrt, z, xlt)
+        def xstep(dz, up=False):
+            a, b = (xlt, xrt) if up else (xrt, xlt)
+            have(zp[dz], a)
+            fwd(zp[dz], a, z, b)
 
         spread(z)
         have(zp[7], x)
@@ -316,20 +317,24 @@
         fwd(zp[2], x, zl, x)
         spread(zp[6])
         spread(zp[2])
-        xstep(0)
+        xstep(0, True)
         xstep(7)
-        xstep(1)
-        for dz in (5, 3, 4):
+        xstep(1, True)
+        have(zp[4], x)
+        spread(zp[4], True)
+        for dz in (5, 3):
             have(zp[dz], x)
-            spread(zp[dz], True)
+            spread(zp[dz])
         xstep(6)
         xstep(2)
         weights()
         front1(x)
-        for dz in (3, 4, 5):
+        xstep(5, True)
+        xstep(3)
+        for dz in (0, 1, 4, 5):
             have(zp[dz], xrt)
         front1(xrt)
-        for dz in range(NZ):
+        for dz in (7, 6, 2, 3, 4):
             have(zp[dz], xlt)
         front1(xlt)
         for dz in range(NZ):
@@ -360,14 +365,22 @@
 
     lax.fori_loop(0, 4, middle, 0)
     blk = c * 4 + y
-    for i in range(4):
+    def give_hidden(i):
         qh = m4(z + (0, 3, 1, 2)[i])
+        for dy in (2, 1, 3, 0):
+            send(hb.at[qh], hall.at[blk, qh], 8, hallr.at[c * 4 + qh], fid(x, z, 0), yp[dy],
+                 own=(c == 0) if dy == 0 else None)
+
+    def give_grads(i):
         qg = m4(y + 8 - x - (2, 1, 3, 0)[i])
         for dy in (2, 1, 3, 0):
             send(gb.at[qg], gall.at[blk, qg], 7, hallr.at[m4(y + 4 - qg)], fid(x, z, 1), yp[dy],
                  own=(c == 1) if dy == 0 else None)
-            send(hb.at[qh], hall.at[blk, qh], 8, hallr.at[c * 4 + qh], fid(x, z, 0), yp[dy],
-                 own=(c == 0) if dy == 0 else None)
+
+    for fn, i in (
+        (give_hidden, 0), (give_hidden, 1), (give_hidden, 2), (give_grads, 0), (give_grads, 1), (give_grads, 2), (give_hidden, 3), (give_grads, 3),
+    ):
+        fn(i)
 
     def small_a():
         mids = jnp.zeros((64, EX), F32)
@@ -380,6 +393,8 @@
         sp[:, :, EX : 2 * EX] = backs.astype(BF).reshape(4, G, EX)
         for q in range(NX):
             send(sp.at[q], sa.at[x], 9, sar, fid(q, z, c), y, own=x == q)
+
+    small_a()
 
     def small_b():
         wait(sa, sar)
@@ -424,7 +439,6 @@
                     mb.at[cc], fd.at[c], 17, t3r.at[c], fid(x, z, cc), yp[dy],
                     own=(c == cc) if dy == 0 else None,
                 )
-        sent(17, part.at[pl.ds(0, 7), 0])
 
     def order_ext():
         wait(ext, exr)
@@ -479,30 +493,28 @@
         right, left = fid(x, zr, 0), fid(x, zl, 0)
         out0([zf])
         for xx in range(2):
-            ring(0, xx, po[xx * G : (xx + 1) * G, :], right)
-            ring(1, xx + 2, po[(xx + 2) * G : (xx + 3) * G, :], left)
-        small_a()
-        pl.semaphore_wait(zsem, NZ - 1)
+            ring(0, xx, po[xx * G : (xx + 1) * G, :], fid(x, zp[2], 0))
+            ring(1, xx + 2, po[(xx + 2) * G : (xx + 3) * G, :], fid(x, zp[6], 0))
         for s in range(1, 4):
             out0([zp[4 - s], zp[4 + s]])
             for xx in range(NX):
-                v = po[xx * G : (xx + 1) * G, :]
-                if s > 1 or xx < 2:
-                    v = v + come(0, (s - 1) * 4 + xx)
-                ring(0, s * 4 + xx, v, right)
-                v = po[(4 + xx) * G : (5 + xx) * G, :]
-                if s > 1 or xx >= 2:
-                    v = v + come(1, (s - 1) * 4 + xx)
-                ring(1, s * 4 + xx, v, left)
+                for d, tgt in ((0, right), (1, left)):
+                    v = po[(4 * d + xx) * G : (4 * d + xx + 1) * G, :]
+                    if s > 1:
+                        v = v + come(d, (s - 1) * 4 + xx)
+                    if s == 2 and xx // 2 == d:
+                        v = v + come(d, xx)
+                    ring(d, s * 4 + xx, v, tgt)
             (small_b, small_c, small_d)[s - 1]()
         out0([z])
-        for xx in range(NX):
-            v = po[xx * G : (xx + 1) * G, :] + come(0, 12 + xx) + come(1, 12 + xx)
-            last(xx, v, dlv, xx, z, x == xx, rows0, rowss.at[0], x)
+        pl.semaphore_wait(zsem, NZ - 1)
         order_ext()
         for b in range(2):
             dlp[b] = mm_tn(extp[...], hall[:, :, b].reshape(512, H))[0:R]
         send(dlp.at[1], dlr.at[0], 15, lar.at[0], sib, y)
+        for xx in range(NX):
+            v = po[xx * G : (xx + 1) * G, :] + come(0, 12 + xx) + come(1, 12 + xx)
+            last(xx, v, dlv, xx, z, x == xx, rows0, rowss.at[0], x)
         pl.when(x == y)(small_e)
         sent(4, rsr.at[pl.ds(0, 28)])
         sent(6, part.at[pl.ds(0, 7)])
@@ -511,6 +523,7 @@
         sent(14, rsr.at[pl.ds(0, 28)])
         sent(15, dlp.at[0])
         sent(16, msg.at[pl.ds(0, 31)])
+        pl.when(x == y)(lambda: sent(17, part.at[pl.ds(0, 7), 0]))
 
     def out1(t, dst):
         wait(gall.at[:, 0], hallr.at[t])
@@ -536,8 +549,6 @@
         for zz in range(4):
             ring(0, zz, po[zz * G : (zz + 1) * G, :], right)
             ring(1, zz + 4, po[(zz + 4) * G : (zz + 5) * G, :], left)
-        small_a()
-        pl.semaphore_wait(zsem, NZ - 1)
         out1(xrt, po)
         for zz in range(4, 8):
             ring(0, 8 + zz, po[zz * G : (zz + 1) * G, :], right)
@@ -549,11 +560,13 @@
             ring(1, 12 + zz, pq[(zz + 4) * G : (zz + 5) * G, :] + come(1, zz + 4), left)
         small_b()
         out1(x, po)
+        pl.semaphore_wait(zsem, NZ - 1)
         small_c()
-        for zz in (0, 4, 1, 5, 2, 6, 3, 7):
+        for i, zz in enumerate((0, 4, 1, 5, 2, 6, 3, 7)):
             v = po[zz * G : (zz + 1) * G, :] + come(0, 8 + zz) + come(1, 8 + zz)
             last(zz, v, gev, x, zz, z == zz, rows1, rowss.at[1], z)
-        small_d()
+            if i == 3:
+                small_d()
         order_ext()
         for b in range(4):
             grad = mm_tn(extp[...], gall[:, :, b].reshape(512, H))
@@ -568,6 +581,7 @@
         sent(14, rsr.at[pl.ds(0, 24)])
         sent(15, dlp.at[pl.ds(0, 2)])
         sent(16, msg.at[pl.ds(0, 63)])
+        pl.when(x == y)(lambda: sent(17, part.at[pl.ds(0, 7), 0]))
 
     pl.when(c == 0)(scatter0)
     pl.when(c == 1)(scatter1)

time: 76.3 us -> 73.8 us (0.967)
  Pallas kernels: 75 us -> 73.1 us
    pallas_call x1, Pallas kernels: 73.2 us -> 71.3 us  [on_device(): pl.pallas_call(kernel, out_shape=[S((2, NY, G, H), F32), S((2, EX, EX), B...]
where the time goes in v4:
time: 73.8 us; the launch traced here: 73.7 us
  Pallas kernels  73.1 us (99%)
    pallas_call x1, Pallas kernels, on_device(): pl.pallas_call(kernel, out_shape=[S((2, NY, G, H), F32), S((2, EX, EX), B...  71.3 us
    pallas_call x1, Pallas kernels, on_device(): pl.pallas_call(place, out_shape=[S((2, NY * KP), BF), S((2, NY * KP), BF)...  1.83 us

profile of v4, /device:TPU:7, one launch (start us, length us, event | category | flops | bytes accessed | tf_op | source)
XLA Modules:
  0.0 73.7 jit_solution(10593273775234238124)
XLA Ops:
  0.6 71.3 %lora_ffn_step.1 = (f32[2,4,16,256]{3,2,1,0:T(8,128)}, bf16[2,128,128]{2,1,0:T(8,128)(2,1)}, f32[3,64,256]{2,1,0:T(8,128)}) custom-call(bf16[2,7168]{1,0:T(2,128)(2,1)} %tok_hbm.1, bf16[2,7168]{1,0:T(2,128)(2,1)} %gout_hbm.1, bf16[2,14]{1,0:T(2,128)(2,1)} %bitcast.11, bf16[2,14]{1,0:T(2,128)(2,1)} %bitcast.12, bf16[2,14]{1,0:T(2,128)(2,1)} %ds_hbm.1, ...), custom_call_target="tpu_custom_call" | custom-call | tf_op jit(solution)/shard_map/lora_ffn_step/pallas_call | solution.py:679
  71.9 1.8 %place_outputs.1 = (bf16[2,7168]{1,0:T(2,128)(2,1)}, bf16[2,7168]{1,0:T(2,128)(2,1)}, f32[64,112]{1,0:T(8,128)}, f32[64,256]{1,0:T(8,128)}, f32[64,112]{1,0:T(8,...) custom-call(f32[2,4,16,256]{3,2,1,0:T(8,128)} %get-tuple-element.19.rows_ref, ...), custom_call_target="tpu_custom_call" | custom-call | tf_op jit(solution)/shard_map/place_outputs/pallas_call | solution.py:693

commit v5 on v4

--- a/solution.py
+++ b/solution.py
@@ -278,11 +278,15 @@
             za, zb = zp[8 - k], zp[k]
             for i, xx in enumerate((x, xrt, xlt, xf)):
                 have(za, xx)
-                if k < 3 or i < 1:
+                if k < 3:
                     fwd(za, xx, zr, x)
+                if k == 2 and i < 2:
+                    fwd(za, xx, zp[2], x)
                 have(zb, xx)
-                if k < 3 or i >= 1:
+                if k < 3:
                     fwd(zb, xx, zl, x)
+                if k == 2 and i >= 2:
+                    fwd(zb, xx, zp[6], x)
             front0([za, zb])
         for xx in range(NX):
             have(zf, xx)
@@ -516,14 +520,6 @@
             v = po[xx * G : (xx + 1) * G, :] + come(0, 12 + xx) + come(1, 12 + xx)
             last(xx, v, dlv, xx, z, x == xx, rows0, rowss.at[0], x)
         pl.when(x == y)(small_e)
-        sent(4, rsr.at[pl.ds(0, 28)])
-        sent(6, part.at[pl.ds(0, 7)])
-        sent(7, part.at[pl.ds(0, 4)])
-        sent(8, part.at[pl.ds(0, 3), pl.ds(0, 2)])
-        sent(14, rsr.at[pl.ds(0, 28)])
-        sent(15, dlp.at[0])
-        sent(16, msg.at[pl.ds(0, 31)])
-        pl.when(x == y)(lambda: sent(17, part.at[pl.ds(0, 7), 0]))
 
     def out1(t, dst):
         wait(gall.at[:, 0], hallr.at[t])
@@ -574,14 +570,6 @@
         send(dlp.at[0], dlr.at[0], 15, lar.at[0], sib, y)
         send(dlp.at[2], dlr.at[1], 15, lar.at[1], sib, y)
         pl.when(x == y)(small_e)
-        sent(4, rsr.at[pl.ds(0, 31)])
-        sent(6, part.at[pl.ds(0, 7), pl.ds(0, 2)])
-        sent(7, part.at[pl.ds(0, 3)])
-        sent(8, part.at[pl.ds(0, 2)])
-        sent(14, rsr.at[pl.ds(0, 24)])
-        sent(15, dlp.at[pl.ds(0, 2)])
-        sent(16, msg.at[pl.ds(0, 63)])
-        pl.when(x == y)(lambda: sent(17, part.at[pl.ds(0, 7), 0]))
 
     pl.when(c == 0)(scatter0)
     pl.when(c == 1)(scatter1)
@@ -604,13 +592,31 @@
         for i in range(1, n):
             v += rows[i].astype(F32)
         rowsf[kind] = v
-    out_rows = pltpu.make_async_copy(rowsf, rows_out, outsem.at[4])
-    out_rows.start()
-    for i in range(3):
-        wait(dlp.at[0], outsem.at[i])
-    out_fd.wait()
-    out_rows.wait()
+        pltpu.make_async_copy(rowsf.at[kind], rows_out.at[kind], outsem.at[4 + kind]).start()
     sent(0, msg.at[pl.ds(0, 19)])
+
+    @pl.when(c == 0)
+    def _():
+        sent(4, rsr.at[pl.ds(0, 28)])
+        sent(6, part.at[pl.ds(0, 7)])
+        sent(7, part.at[pl.ds(0, 4)])
+        sent(8, part.at[pl.ds(0, 3), pl.ds(0, 2)])
+        sent(14, rsr.at[pl.ds(0, 28)])
+        sent(15, dlp.at[0])
+        sent(16, msg.at[pl.ds(0, 31)])
+        pl.when(x == y)(lambda: sent(17, part.at[pl.ds(0, 7), 0]))
+
+    @pl.when(c == 1)
+    def _():
+        sent(4, rsr.at[pl.ds(0, 31)])
+        sent(6, part.at[pl.ds(0, 7), pl.ds(0, 2)])
+        sent(7, part.at[pl.ds(0, 3)])
+        sent(8, part.at[pl.ds(0, 2)])
+        sent(14, rsr.at[pl.ds(0, 24)])
+        sent(15, dlp.at[pl.ds(0, 2)])
+        sent(16, msg.at[pl.ds(0, 63)])
+        pl.when(x == y)(lambda: sent(17, part.at[pl.ds(0, 7), 0]))
+
     sent(1, wgu.at[0])
     sent(2, wgu.at[0])
     sent(3, wd.at[0])
@@ -622,6 +628,11 @@
         @pl.when(jnp.logical_not(jnp.logical_and(c == cc, y == x)))
         def _(cc=cc):
             sent(12 + cc, smm.at[0])
+    for i in range(3):
+        wait(dlp.at[0], outsem.at[i])
+    out_fd.wait()
+    for kind in range(2):
+        wait(rowsf.at[kind], outsem.at[4 + kind])
 
 
 def place(rows_ref, fd_ref, dla_ref, lo, gt, dget, dgl, duet, dul, ddet, ddl, row):
@@ -668,7 +679,7 @@
         V((4, 4, G, H), BF), V((8, 4, 4, G, H), BF),
         V((128, KE), F32), V((128, KE), F32), V((32, G, KE), BF), V((32, G, KE), BF), dma(32),
         V((64, G, H), BF), V((NX, NY, G, H), BF), V((NZ, NY, G, H), BF), dma(2),
-        V((2, NY, G, H), F32), dma(5), V((128, 128), F32), V((128, 128), F32),
+        V((2, NY, G, H), F32), dma(6), V((128, 128), F32), V((128, 128), F32),
         V((4, G, H), BF), V((NX, G, H), BF), one, V((G, H), BF), V((NZ, G, H), BF), one,
         V((G, H), BF), V((NX, G, H), BF), one, V((8, 4, G, EX), BF), one,
         V((384, EX), F32), V((2, EX, EX), BF), V((2, EX, EX), BF), dma(2),

time: 73.8 us -> 73.4 us (level)
  Pallas kernels: 73.1 us -> 72.3 us
    pallas_call x1, Pallas kernels: 71.3 us -> 70.5 us  [on_device(): pl.pallas_call(kernel, out_shape=[S((2, NY, G, H), F32), S((2, EX, EX), B...]
where the time goes in v5:
time: 73.4 us; the launch traced here: 73 us
  Pallas kernels  72.3 us (99%)
    pallas_call x1, Pallas kernels, on_device(): pl.pallas_call(kernel, out_shape=[S((2, NY, G, H), F32), S((2, EX, EX), B...  70.5 us
    pallas_call x1, Pallas kernels, on_device(): pl.pallas_call(place, out_shape=[S((2, NY * KP), BF), S((2, NY * KP), BF)...  1.83 us

profile of v5, /device:TPU:7, one launch (start us, length us, event | category | flops | bytes accessed | tf_op | source)
XLA Modules:
  0.0 73.0 jit_solution(11648120874547496826)
XLA Ops:
  0.6 70.5 %lora_ffn_step.1 = (f32[2,4,16,256]{3,2,1,0:T(8,128)}, bf16[2,128,128]{2,1,0:T(8,128)(2,1)}, f32[3,64,256]{2,1,0:T(8,128)}) custom-call(bf16[2,7168]{1,0:T(2,128)(2,1)} %tok_hbm.1, bf16[2,7168]{1,0:T(2,128)(2,1)} %gout_hbm.1, bf16[2,14]{1,0:T(2,128)(2,1)} %bitcast.11, bf16[2,14]{1,0:T(2,128)(2,1)} %bitcast.12, bf16[2,14]{1,0:T(2,128)(2,1)} %ds_hbm.1, ...), custom_call_target="tpu_custom_call" | custom-call | tf_op jit(solution)/shard_map/lora_ffn_step/pallas_call | solution.py:690
  71.2 1.8 %place_outputs.1 = (bf16[2,7168]{1,0:T(2,128)(2,1)}, bf16[2,7168]{1,0:T(2,128)(2,1)}, f32[64,112]{1,0:T(8,128)}, f32[64,256]{1,0:T(8,128)}, f32[64,112]{1,0:T(8,...) custom-call(f32[2,4,16,256]{3,2,1,0:T(8,128)} %get-tuple-element.19.rows_ref, ...), custom_call_target="tpu_custom_call" | custom-call | tf_op jit(solution)/shard_map/place_outputs/pallas_call | solution.py:704

commit v6 on v5

--- a/solution.py
+++ b/solution.py
@@ -211,7 +211,7 @@
         wait(st1.at[xx], s1r.at[xx])
         got = st1[xx].reshape(128, H).astype(F32)
         for h, part_ref in enumerate((gota, gotb)):
-            part_ref[...] = got[:, h * 128 : (h + 1) * 128]
+            part_ref[0:128, :] = got[:, h * 128 : (h + 1) * 128]
             for j in range(8 - h):
                 k = 2 * j + h
                 aa[z, xx, :, k * 128 : (k + 1) * 128] = part_ref[pl.ds(j, G, stride=8), :].astype(BF)
@@ -468,8 +468,8 @@
         for j in range(7):
             gota[pl.ds(j, G, stride=8), :] = v[:, j * 256 : j * 256 + 128]
             gotb[pl.ds(j, G, stride=8), :] = v[:, j * 256 + 128 : (j + 1) * 256]
-        msg[g * 8 : (g + 1) * 8, :, 0:128] = gota[...].astype(BF).reshape(8, G, 128)
-        msg[g * 8 : (g + 1) * 8, :, 128:256] = gotb[...].astype(BF).reshape(8, G, 128)
+        msg[g * 8 : (g + 1) * 8, :, 0:128] = gota[0:128, :].astype(BF).reshape(8, G, 128)
+        msg[g * 8 : (g + 1) * 8, :, 128:256] = gotb[0:128, :].astype(BF).reshape(8, G, 128)
         for dy in (2, 1, 3, 0):
             for cc in range(2):
                 send(
@@ -679,7 +679,7 @@
         V((4, 4, G, H), BF), V((8, 4, 4, G, H), BF),
         V((128, KE), F32), V((128, KE), F32), V((32, G, KE), BF), V((32, G, KE), BF), dma(32),
         V((64, G, H), BF), V((NX, NY, G, H), BF), V((NZ, NY, G, H), BF), dma(2),
-        V((2, NY, G, H), F32), dma(6), V((128, 128), F32), V((128, 128), F32),
+        V((2, NY, G, H), F32), dma(6), V((136, 128), F32), V((136, 128), F32),
         V((4, G, H), BF), V((NX, G, H), BF), one, V((G, H), BF), V((NZ, G, H), BF), one,
         V((G, H), BF), V((NX, G, H), BF), one, V((8, 4, G, EX), BF), one,
         V((384, EX), F32), V((2, EX, EX), BF), V((2, EX, EX), BF), dma(2),

time: 73.4 us -> 73.4 us (level)
  no operation moved by 1% of the time
where the time goes in v6:
time: 73.4 us; the launch traced here: 73 us
  Pallas kernels  72.3 us (99%)
    pallas_call x1, Pallas kernels, on_device(): pl.pallas_call(kernel, out_shape=[S((2, NY, G, H), F32), S((2, EX, EX), B...  70.5 us
    pallas_call x1, Pallas kernels, on_device(): pl.pallas_call(place, out_shape=[S((2, NY * KP), BF), S((2, NY * KP), BF)...  1.83 us

profile of v6, /device:TPU:7, one launch (start us, length us, event | category | flops | bytes accessed | tf_op | source)
XLA Modules:
  0.0 73.0 jit_solution(7797703696350157982)
XLA Ops:
  0.6 70.5 %lora_ffn_step.1 = (f32[2,4,16,256]{3,2,1,0:T(8,128)}, bf16[2,128,128]{2,1,0:T(8,128)(2,1)}, f32[3,64,256]{2,1,0:T(8,128)}) custom-call(bf16[2,7168]{1,0:T(2,128)(2,1)} %tok_hbm.1, bf16[2,7168]{1,0:T(2,128)(2,1)} %gout_hbm.1, bf16[2,14]{1,0:T(2,128)(2,1)} %bitcast.11, bf16[2,14]{1,0:T(2,128)(2,1)} %bitcast.12, bf16[2,14]{1,0:T(2,128)(2,1)} %ds_hbm.1, ...), custom_call_target="tpu_custom_call" | custom-call | tf_op jit(solution)/shard_map/lora_ffn_step/pallas_call | solution.py:690
  71.2 1.8 %place_outputs.1 = (bf16[2,7168]{1,0:T(2,128)(2,1)}, bf16[2,7168]{1,0:T(2,128)(2,1)}, f32[64,112]{1,0:T(8,128)}, f32[64,256]{1,0:T(8,128)}, f32[64,112]{1,0:T(8,...) custom-call(f32[2,4,16,256]{3,2,1,0:T(8,128)} %get-tuple-element.19.rows_ref, ...), custom_call_target="tpu_custom_call" | custom-call | tf_op jit(solution)/shard_map/place_outputs/pallas_call | solution.py:704
